TPU v7x, 32 devices: a whole 2x2x4 slice. The times are simulated.
32 devices in a mesh: gx: 4 (over y, x), gy: 8 (over z, core).
Axes of the slice: x: 2, y: 2, z: 4, core: 2. Of those that a mesh axis runs over, the one named last changes fastest.
Arguments:
- velocity_u: float32 [16, 64, 1024], P(None, 'gx', 'gy'), may hold values from -4 to 4
- velocity_v: float32 [16, 64, 1024], P(None, 'gx', 'gy'), may hold values from -4 to 4
- buoyancy: float32 [16, 64, 1024], P(None, 'gx', 'gy'), may hold values from -5 to 5
- surface: float32 [64, 1024], P('gx', 'gy'), may hold values from -0.5 to 0.5
- transport_u: float32 [64, 1024], P('gx', 'gy'), may hold values from -2 to 2
- transport_v: float32 [64, 1024], P('gx', 'gy'), may hold values from -2 to 2
- ocean: int32 [64, 1024], P('gx', 'gy'), may hold values 0 or 1
- layers: int32 [64, 1024], P('gx', 'gy'), may hold values from 4 to 16
Outputs:
- new_u: float32 [16, 64, 1024], P(None, 'gx', 'gy')
- new_v: float32 [16, 64, 1024], P(None, 'gx', 'gy')
- new_buoyancy: float32 [16, 64, 1024], P(None, 'gx', 'gy')
- new_surface: float32 [64, 1024], P('gx', 'gy')
- new_transport_u: float32 [64, 1024], P('gx', 'gy')
- new_transport_v: float32 [64, 1024], P('gx', 'gy')
All inputs are finite; a program needn't handle non-finite values. No bound on the sum of `ocean` on one device may be relied on, other than what follows from the above.
Results may differ from a plain program's by a relative error of at most 0.0001.
Values sent between devices are 32-bit elements; how exact they have to be, the bound alone decides.
A program may use at most 64 MiB of HBM per device.

v0:
```python
import jax
import jax.numpy as jnp
from jax import lax
from jax.experimental import pallas as pl
from jax.experimental.pallas import tpu as pltpu
from jax.sharding import PartitionSpec as P

SUB = 8
STEPS = 2
LANES = 128
ROWS = 16
LEVELS = 16
FIELDS = 3
STACK = FIELDS * LEVELS
MESH = pl.DeviceIdType.MESH
F32 = jnp.float32

DIRS = [(-1, 0), (1, 0), (0, -1), (0, 1), (-1, -1), (-1, 1), (1, -1), (1, 1)]
SIDES = [(-1, -1), (0, -1), (1, -1), (-1, 1), (0, 1), (1, 1)]
MOVING = 2 * LEVELS
CODE_ROW = 2 * STACK
RIM = CODE_ROW + 8
HALF = LANES // 2


RIMS, FORCE, PLANE, EARLY = 0, 1, 2, 3


def turn(x, shift, axis):
    return pltpu.roll(x, shift % x.shape[axis] if isinstance(shift, int) else shift, axis)


def fold(cells):
    low = lax.broadcasted_iota(jnp.int32, (8, LANES), 1) < HALF
    return jnp.where(low, cells[0:8], turn(cells[8:16], HALF, 1))


def unfold(cells):
    return jnp.concatenate([cells, turn(cells, HALF, 1)], axis=0)


def pack_flat(arrays):
    lane = lax.broadcasted_iota(jnp.int32, (ROWS, LANES), 1)
    to_left = to_right = jnp.zeros((ROWS, LANES), F32)
    for a, cells in enumerate(arrays):
        to_right = jnp.where((lane >> 4) == a, turn(cells, 16 * a + 16, 1), to_right)
        to_left = jnp.where((lane >> 4) == a, turn(cells, 16 * a, 1), to_left)
    return fold(to_left), fold(to_right)


def wide(own, up, down, sides, a):
    lane = lax.broadcasted_iota(jnp.int32, (ROWS, LANES), 1)
    blocks = []
    for r in range(3):
        from_left, from_right = unfold(sides[r]), unfold(sides[r + 3])
        left, right = turn(from_left, 112 - 16 * a, 1), turn(from_right, -16 * a, 1)
        blocks.append(jnp.where(lane < 16, right, jnp.where(lane >= 112, left, 0.0)))
    main = jnp.concatenate([up, own, down], axis=0)
    return jnp.concatenate([main, jnp.concatenate(blocks, axis=0)], axis=1)


def barotropic(state, push_u, push_v, code_wide):
    wet = (code_wide > 0.0).astype(F32)
    depth = code_wide / LEVELS
    zero = jnp.zeros((ROWS, LANES), F32)

    def substep(_, carry):
        eta, tu, tv, sum_u, sum_v = carry
        div = (turn(tu, -1, 0) - turn(tu, 1, 0)) + (turn(tv, -1, 1) - turn(tv, 1, 1))
        eta = wet * (eta - 0.125 * div)
        thick = 0.125 * (depth + eta)
        new_u = wet * (
            0.98 * tu + push_u - thick * (turn(eta, -1, 0) - turn(eta, 1, 0)) + 0.05 * tv
        )
        new_v = wet * (
            0.98 * tv + push_v - thick * (turn(eta, -1, 1) - turn(eta, 1, 1)) - 0.05 * tu
        )
        sum_u = sum_u + new_u[ROWS : 2 * ROWS, 0:LANES]
        sum_v = sum_v + new_v[ROWS : 2 * ROWS, 0:LANES]
        return eta, new_u, new_v, sum_u, sum_v

    eta, tu, tv, sum_u, sum_v = lax.fori_loop(
        0, SUB, substep, state + (zero, zero), unroll=True
    )
    own = tuple(c[ROWS : 2 * ROWS, 0:LANES] for c in (eta, tu, tv))
    return own, sum_u, sum_v


def finish_kernel(
    hbm_u, hbm_v, new_b, hbm_columns, hbm_wide,
    out_u, out_v, out_b, out_eta, out_tu, out_tv,
    star_u, star_v, columns, wide_in, buf_u, buf_v, buf_flat, sem, in_sem,
):
    loads = [
        pltpu.make_async_copy(src, dst, in_sem.at[i])
        for i, (src, dst) in enumerate((
            (hbm_wide, wide_in), (hbm_columns, columns), (hbm_u, star_u), (hbm_v, star_v)
        ))
    ]
    for load in loads:
        load.start()
    copies = [pltpu.make_async_copy(new_b, out_b, sem.at[0])]
    copies[0].start()
    loads[0].wait()
    code_wide = wide_in[3]
    own, sum_u, sum_v = barotropic(
        (wide_in[0], wide_in[1], wide_in[2]), wide_in[4], wide_in[5], code_wide
    )
    for a, (cells, out) in enumerate(zip(own, (out_eta, out_tu, out_tv))):
        buf_flat[a] = cells
        copies.append(pltpu.make_async_copy(buf_flat.at[a], out, sem.at[1 + a]))
        copies[-1].start()
    code = code_wide[ROWS : 2 * ROWS, 0:LANES]
    lay = jnp.maximum(code, 1.0)
    scale = LEVELS / SUB
    for load in loads[1:]:
        load.wait()
    for a, (star, buf, out, total) in enumerate(
        ((star_u, buf_u, out_u, sum_u), (star_v, buf_v, out_v, sum_v))
    ):
        shift = (scale * total - columns[a]) / lay

        def finish(k, carry, star=star, buf=buf, shift=shift):
            act = lax.convert_element_type(k, F32) < code
            buf[k] = jnp.where(act, star[k] + shift, 0.0)
            return carry

        lax.fori_loop(0, LEVELS, finish, 0, unroll=True)
        copies.append(pltpu.make_async_copy(buf, out, sem.at[4 + a]))
        copies[-1].start()
    for copy in copies:
        copy.wait()


def kernel(
    vel_u, vel_v, buoy, surface, trans_u, trans_v, ocean, layers,
    hbm_u, hbm_v, hbm_b, hbm_columns, hbm_wide,
    star_u, star_v, out_b, out_columns, out_wide, out_sem,
    fx, lp, dyb, near_ext, code_ext, in_3d, in_2d, in_int,
    x_send, y_send, x_recv, y_recv, gx_send, gy_send, gx_recv, gy_recv,
    fx_send, fy_send, fx_recv, fy_recv, in_sem, send_sem, recv_sem,
):
    loads = []
    for a, ref in enumerate((vel_u, vel_v, buoy)):
        loads.append(pltpu.make_async_copy(ref, in_3d.at[a], in_sem.at[a]))
    for a, ref in enumerate((surface, trans_u, trans_v)):
        loads.append(pltpu.make_async_copy(ref, in_2d.at[a], in_sem.at[3 + a]))
    for a, ref in enumerate((ocean, layers)):
        loads.append(pltpu.make_async_copy(ref, in_int.at[a], in_sem.at[6 + a]))
    for load in loads:
        load.start()
    gx, gy = lax.axis_index("gx"), lax.axis_index("gy")
    nx, ny = lax.axis_size("gx"), lax.axis_size("gy")

    def exists(d):
        ok = jnp.bool_(True)
        if d[0] == -1:
            ok = jnp.logical_and(ok, gx > 0)
        if d[0] == 1:
            ok = jnp.logical_and(ok, gx < nx - 1)
        if d[1] == -1:
            ok = jnp.logical_and(ok, gy > 0)
        if d[1] == 1:
            ok = jnp.logical_and(ok, gy < ny - 1)
        return ok

    here = {d: exists(d) for d in DIRS}
    barrier = pltpu.get_barrier_semaphore()
    total_near = jnp.int32(0)
    for d in DIRS:
        total_near = total_near + here[d].astype(jnp.int32)

        @pl.when(here[d])
        def _(d=d):
            pl.semaphore_signal(barrier, inc=1, device_id=(gx + d[0], gy + d[1]), device_id_type=MESH)

    for d in DIRS:
        @pl.when(jnp.logical_not(here[d]))
        def _(d=d):
            for p in range(STEPS):
                if d[1] == 0:
                    s = 0 if d[0] < 0 else 1
                    x_recv[p, s] = jnp.zeros(x_recv.shape[2:], F32)
                    gx_recv[p, s] = jnp.zeros(gx_recv.shape[2:], F32)
                    fx_recv[p, s] = jnp.zeros(fx_recv.shape[2:], F32)
                else:
                    s = SIDES.index(d)
                    y_recv[p, s] = jnp.zeros(y_recv.shape[2:], F32)
                    gy_recv[p, s] = jnp.zeros(gy_recv.shape[2:], F32)
                    fy_recv[p, s] = jnp.zeros(fy_recv.shape[2:], F32)

    def copies(phase, step):
        result = []
        for i, d in enumerate(DIRS):
            back = (-d[0], -d[1])
            if d[1] == 0:
                src_at, dst_at = (0 if d[0] < 0 else 1), (0 if back[0] < 0 else 1)
                if phase == FORCE:
                    src, dst = fx_send.at[step], fx_recv.at[step, dst_at]
                elif phase == PLANE:
                    rows = pl.ds(0, (4 if step == 0 else 3) * ROWS)
                    src, dst = gx_send.at[step, rows], gx_recv.at[step, dst_at, rows]
                else:
                    if step == 0:
                        rows = pl.ds(0, RIM)
                    elif phase == EARLY:
                        rows = pl.ds(2 * MOVING, 2 * LEVELS)
                    else:
                        rows = pl.ds(0, 2 * MOVING)
                    src, dst = x_send.at[step, src_at, rows], x_recv.at[step, dst_at, rows]
            else:
                src_at, dst_at = (0 if d[1] < 0 else 1), SIDES.index(back)
                if phase == FORCE:
                    src, dst = fy_send.at[step, src_at], fy_recv.at[step, dst_at]
                elif phase == PLANE:
                    src, dst = gy_send.at[step, src_at], gy_recv.at[step, dst_at]
                elif phase == EARLY:
                    continue
                else:
                    src, dst = y_send.at[step, src_at], y_recv.at[step, dst_at]
                    if d[0] != 0:
                        rows = pl.ds(0, 8) if d[0] < 0 else pl.ds(8, 8)
                        src, dst = src.at[rows], dst.at[rows]
            at = phase * STEPS + step
            copy = pltpu.make_async_remote_copy(
                src_ref=src, dst_ref=dst,
                send_sem=send_sem.at[at, i], recv_sem=recv_sem.at[at, DIRS.index(back)],
                device_id=(gx + d[0], gy + d[1]), device_id_type=MESH,
            )
            result.append((d, copy))
        return result

    def start(phase, step):
        for d, copy in copies(phase, step):
            @pl.when(here[d])
            def _(copy=copy):
                copy.start()

    def arrive(phase, step):
        by_dir = dict(copies(phase, step))
        for d in by_dir:
            @pl.when(here[d])
            def _(d=d):
                by_dir[(-d[0], -d[1])].wait_recv()

    def sent(phase, step):
        for d, copy in copies(phase, step):
            @pl.when(here[d])
            def _(copy=copy):
                copy.wait_send()

    lane = lax.broadcasted_iota(jnp.int32, (ROWS, LANES), 1)
    pair = lane >> 1
    odd = (lane & 1) == 1
    zero = jnp.zeros((ROWS, LANES), F32)

    def put(step, j, near_at, far_at, cells, strips):
        x_send[step, 0, pl.ds(near_at, 1)] = cells[0:1]
        x_send[step, 0, pl.ds(far_at, 1)] = cells[1:2]
        x_send[step, 1, pl.ds(near_at, 1)] = cells[ROWS - 1 : ROWS]
        x_send[step, 1, pl.ds(far_at, 1)] = cells[ROWS - 2 : ROWS - 1]
        to_left, to_right = strips
        rolled = turn(cells, 2 * j + 2, 1)
        to_right = jnp.where(pair == j, rolled, to_right)
        to_left = jnp.where(pair == j + 1, rolled, to_left)
        return to_left, to_right

    def put_v(step, j, cells, strips):
        fx[j, pl.ds(2, ROWS)] = cells
        return put(step, j, j, MOVING + j, cells, strips)

    def put_b(step, k, cells, strips):
        j = MOVING + k
        return put(step, j, 2 * MOVING + k, 2 * MOVING + LEVELS + k, cells, strips)

    def send_state(step, strips, flats):
        y_send[step, 0] = strips[0]
        y_send[step, 1] = strips[1]
        start(RIMS, step)
        flat_left, flat_right = pack_flat(flats)
        gy_send[step, 0] = flat_left
        gy_send[step, 1] = flat_right
        for a, cells in enumerate(flats):
            gx_send[step, ROWS * a : ROWS * (a + 1)] = cells
        start(PLANE, step)

    loads[6].wait()
    loads[7].wait()
    lay = in_int[1].astype(F32)
    code = jnp.where(in_int[0] > 0, lay, 0.0)
    strips = put(0, STACK, CODE_ROW, CODE_ROW + 1, code, (zero, zero))
    for a in range(FIELDS):
        loads[a].wait()

        def pack(k, strips, a=a):
            cells = in_3d[a, k]
            if a < 2:
                return put_v(0, a * LEVELS + k, cells, strips)
            fx[MOVING + k, pl.ds(2, ROWS)] = cells
            return put_b(0, k, cells, strips)

        strips = lax.fori_loop(0, LEVELS, pack, strips, unroll=True)
    for a in range(3):
        loads[3 + a].wait()
    pl.semaphore_wait(barrier, total_near)
    sea, flow_u, flow_v = in_2d[0], in_2d[1], in_2d[2]
    send_state(0, strips, (sea, flow_u, flow_v, code))

    lane18 = lax.broadcasted_iota(jnp.int32, (ROWS + 2, LANES), 1)
    for step in range(STEPS):
        arrive(RIMS, step)
        if step:
            arrive(EARLY, step)
        from_left, from_right = y_recv[step, 1], y_recv[step, 4]
        near = jnp.where(odd, from_left, turn(from_right, -2, 1))
        far = jnp.where(odd, turn(from_left, 1, 1), turn(from_right, -3, 1))
        inner = turn(jnp.where(odd, strips[1], strips[0]), -1, 1)
        near_ext[pl.ds(1, ROWS)] = near
        odd8 = odd[0:8]
        top = jnp.where(odd8, y_recv[step, 0, 8:16], turn(y_recv[step, 3, 8:16], -2, 1))
        low = jnp.where(odd8, y_recv[step, 2, 0:8], turn(y_recv[step, 5, 0:8], -2, 1))
        near_ext[pl.ds(0, 1)] = top[7:8]
        near_ext[pl.ds(ROWS + 1, 1)] = low[0:1]

        if step == 0:
            code_ext[pl.ds(0, 1)] = x_recv[0, 0, pl.ds(CODE_ROW, 1)]
            code_ext[pl.ds(1, ROWS)] = code
            code_ext[pl.ds(ROWS + 1, 1)] = x_recv[0, 1, pl.ds(CODE_ROW, 1)]
            at = 2 * STACK
            code_near = jnp.where(
                odd,
                jnp.broadcast_to(near[:, at + 1 : at + 2], (ROWS, LANES)),
                jnp.broadcast_to(near[:, at : at + 1], (ROWS, LANES)),
            )
            act_near = ((pair & (LEVELS - 1)).astype(F32) < code_near).astype(F32)
            code18 = code_ext[pl.ds(0, ROWS + 2)]
        lap_near = act_near * (
            far + inner + near_ext[pl.ds(0, ROWS)] + near_ext[pl.ds(2, ROWS)] - 4.0 * near
        )
        near18 = near_ext[pl.ds(0, ROWS + 2)]

        def biharm(j, near_at, far_at, act18):
            fx[j, pl.ds(0, 1)] = x_recv[step, 0, pl.ds(far_at, 1)]
            fx[j, pl.ds(1, 1)] = x_recv[step, 0, pl.ds(near_at, 1)]
            fx[j, pl.ds(ROWS + 2, 1)] = x_recv[step, 1, pl.ds(near_at, 1)]
            fx[j, pl.ds(ROWS + 3, 1)] = x_recv[step, 1, pl.ds(far_at, 1)]
            mid = fx[j, pl.ds(1, ROWS + 2)]
            edge = turn(near18, 127 - 2 * j, 1)
            ahead = jnp.where(lane18 == LANES - 1, edge, turn(mid, -1, 1))
            behind = jnp.where(lane18 == 0, edge, turn(mid, 1, 1))
            lap = act18 * (
                fx[j, pl.ds(0, ROWS + 2)] + fx[j, pl.ds(2, ROWS + 2)] + ahead + behind - 4.0 * mid
            )
            lp[j, pl.ds(0, ROWS + 2)] = lap
            mid = lp[j, pl.ds(1, ROWS)]
            edge = turn(lap_near, 127 - 2 * j, 1)
            ahead = jnp.where(lane == LANES - 1, edge, turn(mid, -1, 1))
            behind = jnp.where(lane == 0, edge, turn(mid, 1, 1))
            return lp[j, pl.ds(0, ROWS)] + lp[j, pl.ds(2, ROWS)] + ahead + behind - 4.0 * mid

        def buoyancy(k, carry):
            level_at = lax.convert_element_type(k, F32)
            act18 = (level_at < code18).astype(F32)
            act = (level_at < code).astype(F32)
            at = 2 * LEVELS + k
            bih_b = biharm(at, 2 * MOVING + k, 2 * MOVING + LEVELS + k, act18)
            u, v = fx[k, pl.ds(2, ROWS)], fx[LEVELS + k, pl.ds(2, ROWS)]
            b = fx[at, pl.ds(2, ROWS)]
            b_x = fx[at, pl.ds(3, ROWS)] - fx[at, pl.ds(1, ROWS)]
            tend_b = -0.5 * (u * b_x + v * dyb[k, pl.ds(0, ROWS)]) - 0.02 * bih_b
            new_b = act * (b + 0.2 * tend_b)
            if step == STEPS - 1:
                out_b[k] = new_b
            else:
                fx[at, pl.ds(2, ROWS)] = new_b
            return carry

        def level(k, carry):
            press_x, press_y, force_u, force_v, col_u, col_v = carry
            level_at = lax.convert_element_type(k, F32)
            act18 = (level_at < code18).astype(F32)
            act = (level_at < code).astype(F32)
            bih_u = biharm(k, k, MOVING + k, act18)
            bih_v = biharm(LEVELS + k, LEVELS + k, MOVING + LEVELS + k, act18)
            u, v = fx[k, pl.ds(2, ROWS)], fx[LEVELS + k, pl.ds(2, ROWS)]
            at = 2 * LEVELS + k
            fx[at, pl.ds(1, 1)] = x_recv[step, 0, pl.ds(2 * MOVING + k, 1)]
            fx[at, pl.ds(ROWS + 2, 1)] = x_recv[step, 1, pl.ds(2 * MOVING + k, 1)]
            b = fx[at, pl.ds(2, ROWS)]
            edge = turn(near, 127 - 2 * at, 1)
            b_x = fx[at, pl.ds(3, ROWS)] - fx[at, pl.ds(1, ROWS)]
            b_y = jnp.where(lane == LANES - 1, edge, turn(b, -1, 1)) - jnp.where(
                lane == 0, edge, turn(b, 1, 1)
            )
            dyb[k, pl.ds(0, ROWS)] = b_y
            press_x, press_y = press_x + b_x, press_y + b_y
            tend_u = (-0.25 / LEVELS) * press_x + 0.1 * v - 0.02 * bih_u
            tend_v = (-0.25 / LEVELS) * press_y - 0.1 * u - 0.02 * bih_v
            su = act * (u + 0.2 * tend_u)
            sv = act * (v + 0.2 * tend_v)
            star_u[k] = su
            star_v[k] = sv
            return (
                press_x, press_y, force_u + act * tend_u, force_v + act * tend_v,
                col_u + su, col_v + sv,
            )

        _, _, force_u, force_v, col_u, col_v = lax.fori_loop(
            0, LEVELS, level, (zero,) * 6, unroll=True
        )
        force_u, force_v = force_u / LEVELS, force_v / LEVELS
        fx_send[step, 0:ROWS] = force_u
        fx_send[step, ROWS : 2 * ROWS] = force_v
        flat_left, flat_right = pack_flat((force_u, force_v))
        fy_send[step, 0] = flat_left
        fy_send[step, 1] = flat_right
        start(FORCE, step)
        lax.fori_loop(0, LEVELS, buoyancy, 0, unroll=True)
        if step == STEPS - 1:
            out_columns[0] = col_u
            out_columns[1] = col_v
            stores = [
                pltpu.make_async_copy(src, dst, out_sem.at[i])
                for i, (src, dst) in enumerate((
                    (star_u, hbm_u), (star_v, hbm_v), (out_b, hbm_b), (out_columns, hbm_columns),
                    (out_wide.at[0:4], hbm_wide.at[0:4]), (out_wide.at[4:6], hbm_wide.at[4:6]),
                ))
            ]
            for store in stores[:4]:
                store.start()

        if step < STEPS - 1:
            def pack_b(k, strips):
                return put_b(step + 1, k, fx[MOVING + k, pl.ds(2, ROWS)], strips)

            strips = lax.fori_loop(0, LEVELS, pack_b, (zero, zero), unroll=True)
            start(EARLY, step + 1)
        arrive(PLANE, step)
        sides = [gy_recv[step, r] for r in range(6)]

        def plane(own, a):
            rows = slice(ROWS * a, ROWS * (a + 1))
            return wide(own, gx_recv[step, 0, rows], gx_recv[step, 1, rows], sides, a)

        if step == 0:
            code_wide = plane(code, 3)
        state = (plane(sea, 0), plane(flow_u, 1), plane(flow_v, 2))
        if step == STEPS - 1:
            for a, cells in enumerate(state + (code_wide,)):
                out_wide[a] = cells
            stores[4].start()
        arrive(FORCE, step)
        sides_f = [fy_recv[step, r] for r in range(6)]
        push_u, push_v = (
            0.2 * wide(
                own, fx_recv[step, 0, ROWS * a : ROWS * (a + 1)],
                fx_recv[step, 1, ROWS * a : ROWS * (a + 1)], sides_f, a,
            )
            for a, own in enumerate((force_u, force_v))
        )
        if step == STEPS - 1:
            out_wide[4] = push_u
            out_wide[5] = push_v
            stores[5].start()
        else:
            (sea, flow_u, flow_v), sum_u, sum_v = barotropic(state, push_u, push_v, code_wide)
            scale = LEVELS / SUB
            shift_u = (scale * sum_u - col_u) / lay
            shift_v = (scale * sum_v - col_v) / lay

            def couple(k, strips):
                act = (lax.convert_element_type(k, F32) < code).astype(F32)
                strips = put_v(step + 1, k, act * (star_u[k] + shift_u), strips)
                return put_v(step + 1, LEVELS + k, act * (star_v[k] + shift_v), strips)

            strips = lax.fori_loop(0, LEVELS, couple, strips, unroll=True)
            send_state(step + 1, strips, (sea, flow_u, flow_v))

    for step in range(STEPS):
        for phase in (RIMS, FORCE, PLANE, EARLY):
            if phase != EARLY or step:
                sent(phase, step)
    for store in stores:
        store.wait()


def per_device(velocity_u, velocity_v, buoyancy, surface, transport_u, transport_v, ocean, layers):
    cube = jax.ShapeDtypeStruct(velocity_u.shape, F32)
    flat = jax.ShapeDtypeStruct(surface.shape, F32)
    hbm = pl.BlockSpec(memory_space=pltpu.HBM)
    ext = 24
    columns = jax.ShapeDtypeStruct((2, ROWS, LANES), F32)
    planes = jax.ShapeDtypeStruct((6, 3 * ROWS, 2 * LANES), F32)
    block = (LEVELS, ROWS, LANES)
    middle = pl.pallas_call(
        kernel,
        out_shape=(cube, cube, cube, columns, planes),
        in_specs=[hbm] * 8,
        out_specs=(hbm,) * 5,
        scratch_shapes=[
            pltpu.VMEM(block, F32),
            pltpu.VMEM(block, F32),
            pltpu.VMEM(block, F32),
            pltpu.VMEM(columns.shape, F32),
            pltpu.VMEM(planes.shape, F32),
            pltpu.SemaphoreType.DMA((6,)),
            pltpu.VMEM((STACK, ext, LANES), F32),
            pltpu.VMEM((STACK, ext, LANES), F32),
            pltpu.VMEM((LEVELS, ext, LANES), F32),
            pltpu.VMEM((ext, LANES), F32),
            pltpu.VMEM((ext, LANES), F32),
            pltpu.VMEM((FIELDS,) + block, F32),
            pltpu.VMEM((3, ROWS, LANES), F32),
            pltpu.VMEM((2, ROWS, LANES), jnp.int32),
            pltpu.VMEM((STEPS, 2, RIM, LANES), F32),
            pltpu.VMEM((STEPS, 2, ROWS, LANES), F32),
            pltpu.VMEM((STEPS, 2, RIM, LANES), F32),
            pltpu.VMEM((STEPS, 6, ROWS, LANES), F32),
            pltpu.VMEM((STEPS, 4 * ROWS, LANES), F32),
            pltpu.VMEM((STEPS, 2, 8, LANES), F32),
            pltpu.VMEM((STEPS, 2, 4 * ROWS, LANES), F32),
            pltpu.VMEM((STEPS, 6, 8, LANES), F32),
            pltpu.VMEM((STEPS, 2 * ROWS, LANES), F32),
            pltpu.VMEM((STEPS, 2, 8, LANES), F32),
            pltpu.VMEM((STEPS, 2, 2 * ROWS, LANES), F32),
            pltpu.VMEM((STEPS, 6, 8, LANES), F32),
            pltpu.SemaphoreType.DMA((8,)),
            pltpu.SemaphoreType.DMA((4 * STEPS, 8)),
            pltpu.SemaphoreType.DMA((4 * STEPS, 8)),
        ],
        compiler_params=pltpu.CompilerParams(
            collective_id=0, has_side_effects=True, vmem_limit_bytes=60 * 2**20
        ),
    )(velocity_u, velocity_v, buoyancy, surface, transport_u, transport_v, ocean, layers)
    return tuple(
        pl.pallas_call(
            finish_kernel,
            out_shape=(cube, cube, cube, flat, flat, flat),
            in_specs=[hbm] * 5,
            out_specs=(hbm,) * 6,
            scratch_shapes=[
                pltpu.VMEM(block, F32),
                pltpu.VMEM(block, F32),
                pltpu.VMEM(columns.shape, F32),
                pltpu.VMEM(planes.shape, F32),
                pltpu.VMEM(block, F32),
                pltpu.VMEM(block, F32),
                pltpu.VMEM((3, ROWS, LANES), F32),
                pltpu.SemaphoreType.DMA((6,)),
                pltpu.SemaphoreType.DMA((4,)),
            ],
            compiler_params=pltpu.CompilerParams(vmem_limit_bytes=60 * 2**20),
        )(*middle)
    )


def solution(mesh):
    cube, flat = P(None, "gx", "gy"), P("gx", "gy")
    return jax.shard_map(
        per_device,
        mesh=mesh,
        in_specs=(cube, cube, cube, flat, flat, flat, flat, flat),
        out_specs=(cube, cube, cube, flat, flat, flat),
        check_vma=False,
    )
```

profile of v0, /device:TPU:1, one launch (start us, length us, event | category | flops | bytes accessed | tf_op | source)
XLA Modules:
  0.0 35.3 jit_solution(12392314101511646699)
XLA Ops:
  0.6 29.5 %shard_map.127 = (f32[16,16,128]{2,1,0:T(8,128)}, f32[16,16,128]{2,1,0:T(8,128)}, f32[16,16,128]{2,1,0:T(8,128)}, f32[2,16,128]{2,1,0:T(8,128)}, f32[6,48,256]{2,1,0:T(8,128)}) custom-call(f32[16,16,128]{2,1,0:T(8,128)} %vel_u.1, f32[16,16,128]{2,1,0:T(8,128)} %vel_v.1, f32[16,16,128]{2,1,0:T(8,128)} %buoy.1, f32[16,128]{1,0:T(8,128)} %surface.1, ...), custom_call_target="tpu_custom_call" | custom-call | tf_op jit(solution)/shard_map/pallas_call | solution.py:495
  30.1 5.2 %shard_map.128 = (f32[16,16,128]{2,1,0:T(8,128)}, f32[16,16,128]{2,1,0:T(8,128)}, f32[16,16,128]{2,1,0:T(8,128)}, f32[16,128]{1,0:T(8,128)}, f32[16,128]{1,0:T(8,128)}, /*index=5*/f32[16,128]{1,0:T(8,128)}) custom-call(f32[16,16,128]{2,1,0:T(8,128)} %get-tuple-element.11.hbm_u, f32[16,16,128]{2,1,0:T(8,128)} %get-tuple-element.12.hbm_v, ...), custom_call_target="tpu_custom_call" | custom-call | tf_op jit(solution)/shard_map/pallas_call | solution.py:536
where the time goes:
time: 35.5 us; the launch traced here: 35.3 us
  Pallas kernels  34.6 us (97%)
  between operations  0.64 us (2%)
    pallas_call x1, Pallas kernels, per_device(): pl.pallas_call(kernel, out_shape=(cube, cube, cube, columns, planes), in_...  29.5 us
    pallas_call x1, Pallas kernels, per_device(): pl.pallas_call(finish_kernel, out_shape=(cube, cube, cube, flat, flat, fl...  5.18 us

commit v1 on v0

--- a/solution.py
+++ b/solution.py
@@ -86,56 +86,23 @@
     return own, sum_u, sum_v
 
 
-def finish_kernel(
-    hbm_u, hbm_v, new_b, hbm_columns, hbm_wide,
-    out_u, out_v, out_b, out_eta, out_tu, out_tv,
-    star_u, star_v, columns, wide_in, buf_u, buf_v, buf_flat, sem, in_sem,
-):
-    loads = [
-        pltpu.make_async_copy(src, dst, in_sem.at[i])
-        for i, (src, dst) in enumerate((
-            (hbm_wide, wide_in), (hbm_columns, columns), (hbm_u, star_u), (hbm_v, star_v)
-        ))
+def store_kernel(*refs):
+    count = (len(refs) - 1) // 2
+    sem = refs[-1]
+    copies = [
+        pltpu.make_async_copy(src, dst, sem.at[i])
+        for i, (src, dst) in enumerate(zip(refs[:count], refs[count:-1]))
     ]
-    for load in loads:
-        load.start()
-    copies = [pltpu.make_async_copy(new_b, out_b, sem.at[0])]
-    copies[0].start()
-    loads[0].wait()
-    code_wide = wide_in[3]
-    own, sum_u, sum_v = barotropic(
-        (wide_in[0], wide_in[1], wide_in[2]), wide_in[4], wide_in[5], code_wide
-    )
-    for a, (cells, out) in enumerate(zip(own, (out_eta, out_tu, out_tv))):
-        buf_flat[a] = cells
-        copies.append(pltpu.make_async_copy(buf_flat.at[a], out, sem.at[1 + a]))
-        copies[-1].start()
-    code = code_wide[ROWS : 2 * ROWS, 0:LANES]
-    lay = jnp.maximum(code, 1.0)
-    scale = LEVELS / SUB
-    for load in loads[1:]:
-        load.wait()
-    for a, (star, buf, out, total) in enumerate(
-        ((star_u, buf_u, out_u, sum_u), (star_v, buf_v, out_v, sum_v))
-    ):
-        shift = (scale * total - columns[a]) / lay
-
-        def finish(k, carry, star=star, buf=buf, shift=shift):
-            act = lax.convert_element_type(k, F32) < code
-            buf[k] = jnp.where(act, star[k] + shift, 0.0)
-            return carry
-
-        lax.fori_loop(0, LEVELS, finish, 0, unroll=True)
-        copies.append(pltpu.make_async_copy(buf, out, sem.at[4 + a]))
-        copies[-1].start()
+    for copy in copies:
+        copy.start()
     for copy in copies:
         copy.wait()
 
 
 def kernel(
     vel_u, vel_v, buoy, surface, trans_u, trans_v, ocean, layers,
-    hbm_u, hbm_v, hbm_b, hbm_columns, hbm_wide,
-    star_u, star_v, out_b, out_columns, out_wide, out_sem,
+    out_u, out_v, out_b, out_eta, out_tu, out_tv,
+    star_u, star_v,
     fx, lp, dyb, near_ext, code_ext, in_3d, in_2d, in_int,
     x_send, y_send, x_recv, y_recv, gx_send, gy_send, gx_recv, gy_recv,
     fx_send, fy_send, fx_recv, fy_recv, in_sem, send_sem, recv_sem,
@@ -416,19 +383,6 @@
         fy_send[step, 1] = flat_right
         start(FORCE, step)
         lax.fori_loop(0, LEVELS, buoyancy, 0, unroll=True)
-        if step == STEPS - 1:
-            out_columns[0] = col_u
-            out_columns[1] = col_v
-            stores = [
-                pltpu.make_async_copy(src, dst, out_sem.at[i])
-                for i, (src, dst) in enumerate((
-                    (star_u, hbm_u), (star_v, hbm_v), (out_b, hbm_b), (out_columns, hbm_columns),
-                    (out_wide.at[0:4], hbm_wide.at[0:4]), (out_wide.at[4:6], hbm_wide.at[4:6]),
-                ))
-            ]
-            for store in stores[:4]:
-                store.start()
-
         if step < STEPS - 1:
             def pack_b(k, strips):
                 return put_b(step + 1, k, fx[MOVING + k, pl.ds(2, ROWS)], strips)
@@ -445,10 +399,6 @@
         if step == 0:
             code_wide = plane(code, 3)
         state = (plane(sea, 0), plane(flow_u, 1), plane(flow_v, 2))
-        if step == STEPS - 1:
-            for a, cells in enumerate(state + (code_wide,)):
-                out_wide[a] = cells
-            stores[4].start()
         arrive(FORCE, step)
         sides_f = [fy_recv[step, r] for r in range(6)]
         push_u, push_v = (
@@ -458,16 +408,11 @@
             )
             for a, own in enumerate((force_u, force_v))
         )
-        if step == STEPS - 1:
-            out_wide[4] = push_u
-            out_wide[5] = push_v
-            stores[5].start()
-        else:
-            (sea, flow_u, flow_v), sum_u, sum_v = barotropic(state, push_u, push_v, code_wide)
-            scale = LEVELS / SUB
-            shift_u = (scale * sum_u - col_u) / lay
-            shift_v = (scale * sum_v - col_v) / lay
-
+        (sea, flow_u, flow_v), sum_u, sum_v = barotropic(state, push_u, push_v, code_wide)
+        scale = LEVELS / SUB
+        shift_u = (scale * sum_u - col_u) / lay
+        shift_v = (scale * sum_v - col_v) / lay
+        if step < STEPS - 1:
             def couple(k, strips):
                 act = (lax.convert_element_type(k, F32) < code).astype(F32)
                 strips = put_v(step + 1, k, act * (star_u[k] + shift_u), strips)
@@ -475,35 +420,44 @@
 
             strips = lax.fori_loop(0, LEVELS, couple, strips, unroll=True)
             send_state(step + 1, strips, (sea, flow_u, flow_v))
+        else:
+            def finish(k, carry):
+                act = lax.convert_element_type(k, F32) < code
+                out_u[k] = jnp.where(act, star_u[k] + shift_u, 0.0)
+                out_v[k] = jnp.where(act, star_v[k] + shift_v, 0.0)
+                return carry
+
+            lax.fori_loop(0, LEVELS, finish, 0, unroll=True)
+            out_eta[...] = sea
+            out_tu[...] = flow_u
+            out_tv[...] = flow_v
 
     for step in range(STEPS):
         for phase in (RIMS, FORCE, PLANE, EARLY):
             if phase != EARLY or step:
                 sent(phase, step)
-    for store in stores:
-        store.wait()
 
 
 def per_device(velocity_u, velocity_v, buoyancy, surface, transport_u, transport_v, ocean, layers):
     cube = jax.ShapeDtypeStruct(velocity_u.shape, F32)
     flat = jax.ShapeDtypeStruct(surface.shape, F32)
     hbm = pl.BlockSpec(memory_space=pltpu.HBM)
+    vmem = pl.BlockSpec(memory_space=pltpu.VMEM)
+    outs = (cube, cube, cube, flat, flat, flat)
+    args = [
+        pltpu.with_memory_space_constraint(x, pltpu.HBM)
+        for x in (velocity_u, velocity_v, buoyancy, surface, transport_u, transport_v, ocean, layers)
+    ]
     ext = 24
-    columns = jax.ShapeDtypeStruct((2, ROWS, LANES), F32)
-    planes = jax.ShapeDtypeStruct((6, 3 * ROWS, 2 * LANES), F32)
     block = (LEVELS, ROWS, LANES)
     middle = pl.pallas_call(
         kernel,
-        out_shape=(cube, cube, cube, columns, planes),
+        out_shape=outs,
         in_specs=[hbm] * 8,
-        out_specs=(hbm,) * 5,
+        out_specs=(vmem,) * 6,
         scratch_shapes=[
             pltpu.VMEM(block, F32),
             pltpu.VMEM(block, F32),
-            pltpu.VMEM(block, F32),
-            pltpu.VMEM(columns.shape, F32),
-            pltpu.VMEM(planes.shape, F32),
-            pltpu.SemaphoreType.DMA((6,)),
             pltpu.VMEM((STACK, ext, LANES), F32),
             pltpu.VMEM((STACK, ext, LANES), F32),
             pltpu.VMEM((LEVELS, ext, LANES), F32),
@@ -529,27 +483,17 @@
             pltpu.SemaphoreType.DMA((4 * STEPS, 8)),
         ],
         compiler_params=pltpu.CompilerParams(
-            collective_id=0, has_side_effects=True, vmem_limit_bytes=60 * 2**20
+            collective_id=0, has_side_effects=True, vmem_limit_bytes=16 * 2**20
         ),
-    )(velocity_u, velocity_v, buoyancy, surface, transport_u, transport_v, ocean, layers)
+    )(*args)
     return tuple(
         pl.pallas_call(
-            finish_kernel,
-            out_shape=(cube, cube, cube, flat, flat, flat),
-            in_specs=[hbm] * 5,
+            store_kernel,
+            out_shape=outs,
+            in_specs=[vmem] * 6,
             out_specs=(hbm,) * 6,
-            scratch_shapes=[
-                pltpu.VMEM(block, F32),
-                pltpu.VMEM(block, F32),
-                pltpu.VMEM(columns.shape, F32),
-                pltpu.VMEM(planes.shape, F32),
-                pltpu.VMEM(block, F32),
-                pltpu.VMEM(block, F32),
-                pltpu.VMEM((3, ROWS, LANES), F32),
-                pltpu.SemaphoreType.DMA((6,)),
-                pltpu.SemaphoreType.DMA((4,)),
-            ],
-            compiler_params=pltpu.CompilerParams(vmem_limit_bytes=60 * 2**20),
+            scratch_shapes=[pltpu.SemaphoreType.DMA((6,))],
+            compiler_params=pltpu.CompilerParams(vmem_limit_bytes=16 * 2**20),
         )(*middle)
     )
 

time: 35.5 us -> 31.5 us (0.89)
  Pallas kernels: 34.6 us -> 30.8 us
    pallas_call x2, Pallas kernels: 34.6 us -> 30.8 us  [the longest x1 29.9 us: per_device(): pl.pallas_call(kernel, out_shape=outs, in_specs=[hbm] * 8, out_specs=(vme...]
where the time goes in v1:
time: 31.5 us; the launch traced here: 31.4 us
  Pallas kernels  30.8 us (98%)
  between operations  0.64 us (2%)
    pallas_call x1, Pallas kernels, per_device(): pl.pallas_call(kernel, out_shape=outs, in_specs=[hbm] * 8, out_specs=(vme...  29.9 us
    pallas_call x1, Pallas kernels, per_device(): pl.pallas_call(store_kernel, out_shape=outs, in_specs=[vmem] * 6, out_spe...  0.8 us

profile of v1, /device:TPU:1, one launch (start us, length us, event | category | flops | bytes accessed | tf_op | source)
XLA Modules:
  0.0 31.4 jit_solution(3082308966173107996)
XLA Ops:
  0.6 29.9 %shard_map.127 = (f32[16,16,128]{2,1,0:T(8,128)S(1)}, f32[16,16,128]{2,1,0:T(8,128)S(1)}, f32[16,16,128]{2,1,0:T(8,128)S(1)}, f32[16,128]{1,0:T(8,128)S(1)}, f32...) custom-call(f32[16,16,128]{2,1,0:T(8,128)} %vel_u.1, f32[16,16,128]{2,1,0:T(8,128)} %vel_v.1, f32[16,16,128]{2,1,0:T(8,128)} %buoy.1, ...), custom_call_target="tpu_custom_call" | custom-call | tf_op jit(solution)/shard_map/pallas_call | solution.py:453
  30.6 0.8 %shard_map.128 = (f32[16,16,128]{2,1,0:T(8,128)}, f32[16,16,128]{2,1,0:T(8,128)}, f32[16,16,128]{2,1,0:T(8,128)}, f32[16,128]{1,0:T(8,128)}, f32[16,128]{1,0:T(8,128)}, /*index=5*/f32[16,128]{1,0:T(8,128)}) custom-call(f32[16,16,128]{2,1,0:T(8,128)S(1)} %get-tuple-element.12.refs_0_, f32[16,16,128]{2,1,0:T(8,128)S(1)} %get-tuple-element.13.refs_1_, ...), custom_call_target="tpu_custom_call" | custom-call | tf_op jit(solution)/shard_map/pallas_call | solution.py:490

commit v2 on v1

--- a/solution.py
+++ b/solution.py
@@ -14,6 +14,7 @@
 STACK = FIELDS * LEVELS
 MESH = pl.DeviceIdType.MESH
 F32 = jnp.float32
+BF16 = jnp.bfloat16
 
 DIRS = [(-1, 0), (1, 0), (0, -1), (0, 1), (-1, -1), (-1, 1), (1, -1), (1, 1)]
 SIDES = [(-1, -1), (0, -1), (1, -1), (-1, 1), (0, 1), (1, 1)]
@@ -24,6 +25,8 @@
 
 
 RIMS, FORCE, PLANE, EARLY = 0, 1, 2, 3
+EXT = 32
+OWN = 8
 
 
 def turn(x, shift, axis):
@@ -37,6 +40,28 @@
 
 def unfold(cells):
     return jnp.concatenate([cells, turn(cells, HALF, 1)], axis=0)
+
+
+def split(x):
+    high = x.astype(BF16)
+    return high, (x - high.astype(F32)).astype(BF16)
+
+
+def pick(mask, x):
+    return tuple(jnp.where(mask, part.astype(F32), 0.0).astype(BF16) for part in split(x))
+
+
+def lane_weights():
+    src = lax.broadcasted_iota(jnp.int32, (LANES, LANES), 0)
+    dst = lax.broadcasted_iota(jnp.int32, (LANES, LANES), 1)
+    ahead, behind = (src == dst + 1).astype(F32), (src == dst - 1).astype(F32)
+    odd = (src & 1) == 1
+    first = jnp.logical_and(odd, dst == 0).astype(F32)
+    last = jnp.logical_and(jnp.logical_not(odd), dst == LANES - 1).astype(F32)
+    return [
+        [(ahead + behind).astype(BF16), (ahead - behind).astype(BF16)],
+        [(last + first).astype(BF16), (last - first).astype(BF16)],
+    ]
 
 
 def pack_flat(arrays):
@@ -103,7 +128,8 @@
     vel_u, vel_v, buoy, surface, trans_u, trans_v, ocean, layers,
     out_u, out_v, out_b, out_eta, out_tu, out_tv,
     star_u, star_v,
-    fx, lp, dyb, near_ext, code_ext, in_3d, in_2d, in_int,
+    fx, lp, near_ext, code_ext, in_3d, in_2d, in_int,
+    lane_w, mom_in, buoy_in, mom_out, buoy_out,
     x_send, y_send, x_recv, y_recv, gx_send, gy_send, gx_recv, gy_recv,
     fx_send, fy_send, fx_recv, fy_recv, in_sem, send_sem, recv_sem,
 ):
@@ -233,7 +259,7 @@
         return to_left, to_right
 
     def put_v(step, j, cells, strips):
-        fx[j, pl.ds(2, ROWS)] = cells
+        fx[pl.ds(EXT * j + OWN, ROWS)] = cells
         return put(step, j, j, MOVING + j, cells, strips)
 
     def put_b(step, k, cells, strips):
@@ -251,6 +277,10 @@
             gx_send[step, ROWS * a : ROWS * (a + 1)] = cells
         start(PLANE, step)
 
+    for r, blocks in enumerate(lane_weights()):
+        for c, block in enumerate(blocks):
+            for at in (2 * r, 2 * r + 1):
+                lane_w[LANES * at : LANES * (at + 1), LANES * c : LANES * (c + 1)] = block
     loads[6].wait()
     loads[7].wait()
     lay = in_int[1].astype(F32)
@@ -263,7 +293,7 @@
             cells = in_3d[a, k]
             if a < 2:
                 return put_v(0, a * LEVELS + k, cells, strips)
-            fx[MOVING + k, pl.ds(2, ROWS)] = cells
+            fx[pl.ds(EXT * (MOVING + k) + OWN, ROWS)] = cells
             return put_b(0, k, cells, strips)
 
         strips = lax.fori_loop(0, LEVELS, pack, strips, unroll=True)
@@ -273,7 +303,6 @@
     sea, flow_u, flow_v = in_2d[0], in_2d[1], in_2d[2]
     send_state(0, strips, (sea, flow_u, flow_v, code))
 
-    lane18 = lax.broadcasted_iota(jnp.int32, (ROWS + 2, LANES), 1)
     for step in range(STEPS):
         arrive(RIMS, step)
         if step:
@@ -291,7 +320,6 @@
 
         if step == 0:
             code_ext[pl.ds(0, 1)] = x_recv[0, 0, pl.ds(CODE_ROW, 1)]
-            code_ext[pl.ds(1, ROWS)] = code
             code_ext[pl.ds(ROWS + 1, 1)] = x_recv[0, 1, pl.ds(CODE_ROW, 1)]
             at = 2 * STACK
             code_near = jnp.where(
@@ -300,67 +328,113 @@
                 jnp.broadcast_to(near[:, at : at + 1], (ROWS, LANES)),
             )
             act_near = ((pair & (LEVELS - 1)).astype(F32) < code_near).astype(F32)
-            code18 = code_ext[pl.ds(0, ROWS + 2)]
         lap_near = act_near * (
             far + inner + near_ext[pl.ds(0, ROWS)] + near_ext[pl.ds(2, ROWS)] - 4.0 * near
         )
-        near18 = near_ext[pl.ds(0, ROWS + 2)]
-
-        def biharm(j, near_at, far_at, act18):
-            fx[j, pl.ds(0, 1)] = x_recv[step, 0, pl.ds(far_at, 1)]
-            fx[j, pl.ds(1, 1)] = x_recv[step, 0, pl.ds(near_at, 1)]
-            fx[j, pl.ds(ROWS + 2, 1)] = x_recv[step, 1, pl.ds(near_at, 1)]
-            fx[j, pl.ds(ROWS + 3, 1)] = x_recv[step, 1, pl.ds(far_at, 1)]
-            mid = fx[j, pl.ds(1, ROWS + 2)]
-            edge = turn(near18, 127 - 2 * j, 1)
-            ahead = jnp.where(lane18 == LANES - 1, edge, turn(mid, -1, 1))
-            behind = jnp.where(lane18 == 0, edge, turn(mid, 1, 1))
-            lap = act18 * (
-                fx[j, pl.ds(0, ROWS + 2)] + fx[j, pl.ds(2, ROWS + 2)] + ahead + behind - 4.0 * mid
+
+        def put_parts(ref, at, rows, parts, col):
+            for c, part in enumerate(parts):
+                ref[pl.ds(at, rows), LANES * (col + c) : LANES * (col + c + 1)] = part
+
+        def stage(ref, first, count, source, edge):
+            def one(i, carry):
+                at = pl.multiple_of(ROWS * i, ROWS)
+                cells = source[pl.ds(EXT * (first + i) + OWN, ROWS)]
+                put_parts(ref, at, ROWS, split(cells), 0)
+                put_parts(ref, at, ROWS, pick(pair == first + i, edge), 2)
+                return carry
+
+            lax.fori_loop(0, count, one, 0, unroll=True)
+
+        def rim_rows(ref, first, count, near_at):
+            row = lax.broadcasted_iota(jnp.int32, (count, LANES), 0)
+            group = lax.broadcasted_iota(jnp.int32, (count, LANES), 1) >> 1
+            for side in range(2):
+                cells = x_recv[step, side, pl.ds(near_at, count)]
+                at = ROWS * count + count * side
+                corner = jnp.broadcast_to(
+                    near_ext[pl.ds((ROWS + 1) * side, 1)], (count, LANES)
+                )
+                put_parts(ref, at, count, split(cells), 0)
+                put_parts(ref, at, count, pick(group == first + row, corner), 2)
+                fx[pl.ds(EXT * first + (OWN - 1, OWN + ROWS)[side], count, stride=EXT)] = cells
+
+        def rim_laps(ref, first, count, near_at, far_at):
+            level_of = lax.broadcasted_iota(jnp.int32, (count, LANES), 0) & (LEVELS - 1)
+            for side in range(2):
+                cells = x_recv[step, side, pl.ds(near_at, count)]
+                beside = x_recv[step, side, pl.ds(far_at, count)] + x_send[
+                    step, side, pl.ds(near_at, count)
+                ]
+                lanes_sum = ref[pl.ds(ROWS * count + count * side, count), 0:LANES]
+                code_row = code_ext[pl.ds((ROWS + 1) * side, 1)]
+                lap = jnp.where(
+                    level_of.astype(F32) < code_row, beside + lanes_sum - 4.0 * cells, 0.0
+                )
+                lp[pl.ds(EXT * first + (OWN - 1, OWN + ROWS)[side], count, stride=EXT)] = lap
+
+        def laplace(j, source, lanes_sum):
+            at = EXT * j + OWN
+            return (
+                source[pl.ds(at - 1, ROWS)] + source[pl.ds(at + 1, ROWS)]
+                + lanes_sum - 4.0 * source[pl.ds(at, ROWS)]
             )
-            lp[j, pl.ds(0, ROWS + 2)] = lap
-            mid = lp[j, pl.ds(1, ROWS)]
-            edge = turn(lap_near, 127 - 2 * j, 1)
-            ahead = jnp.where(lane == LANES - 1, edge, turn(mid, -1, 1))
-            behind = jnp.where(lane == 0, edge, turn(mid, 1, 1))
-            return lp[j, pl.ds(0, ROWS)] + lp[j, pl.ds(2, ROWS)] + ahead + behind - 4.0 * mid
+
+        def own_laps(ref, first, count):
+            def one(i, carry):
+                level_at = lax.convert_element_type(i & (LEVELS - 1), F32)
+                lanes_sum = ref[pl.ds(pl.multiple_of(ROWS * i, ROWS), ROWS), 0:LANES]
+                lap = laplace(first + i, fx, lanes_sum)
+                lp[pl.ds(EXT * (first + i) + OWN, ROWS)] = jnp.where(level_at < code, lap, 0.0)
+                return carry
+
+            lax.fori_loop(0, count, one, 0, unroll=True)
+
+        def apply(source, rows, width):
+            return jnp.dot(
+                source[0:rows], lane_w[:, 0:width], preferred_element_type=F32
+            )
+
+        rows_uv, rows_b = MOVING * ROWS, LEVELS * ROWS
+        rim_rows(buoy_in, MOVING, LEVELS, 2 * MOVING)
+        stage(buoy_in, MOVING, LEVELS, fx, near)
+        buoy_out[...] = apply(buoy_in, rows_b + 2 * LEVELS, 2 * LANES)
+        rim_rows(mom_in, 0, MOVING, 0)
+        stage(mom_in, 0, MOVING, fx, near)
+        mom_out[...] = apply(mom_in, rows_uv + 2 * MOVING, LANES)
+        rim_laps(mom_out, 0, MOVING, 0, MOVING)
+        own_laps(mom_out, 0, MOVING)
+        stage(mom_in, 0, MOVING, lp, lap_near)
+        mom_out[0:rows_uv] = apply(mom_in, rows_uv, LANES)
 
         def buoyancy(k, carry):
-            level_at = lax.convert_element_type(k, F32)
-            act18 = (level_at < code18).astype(F32)
-            act = (level_at < code).astype(F32)
-            at = 2 * LEVELS + k
-            bih_b = biharm(at, 2 * MOVING + k, 2 * MOVING + LEVELS + k, act18)
-            u, v = fx[k, pl.ds(2, ROWS)], fx[LEVELS + k, pl.ds(2, ROWS)]
-            b = fx[at, pl.ds(2, ROWS)]
-            b_x = fx[at, pl.ds(3, ROWS)] - fx[at, pl.ds(1, ROWS)]
-            tend_b = -0.5 * (u * b_x + v * dyb[k, pl.ds(0, ROWS)]) - 0.02 * bih_b
-            new_b = act * (b + 0.2 * tend_b)
+            act = lax.convert_element_type(k, F32) < code
+            at = EXT * (MOVING + k) + OWN
+            rows = pl.ds(pl.multiple_of(ROWS * k, ROWS), ROWS)
+            bih_b = laplace(MOVING + k, lp, buoy_out[rows, 0:LANES])
+            u, v = fx[pl.ds(EXT * k + OWN, ROWS)], fx[pl.ds(EXT * (LEVELS + k) + OWN, ROWS)]
+            b = fx[pl.ds(at, ROWS)]
+            b_x = fx[pl.ds(at + 1, ROWS)] - fx[pl.ds(at - 1, ROWS)]
+            b_y = buoy_out[rows, LANES : 2 * LANES]
+            tend_b = -0.5 * (u * b_x + v * b_y) - 0.02 * bih_b
+            new_b = jnp.where(act, b + 0.2 * tend_b, 0.0)
             if step == STEPS - 1:
                 out_b[k] = new_b
             else:
-                fx[at, pl.ds(2, ROWS)] = new_b
+                in_3d[2, k] = new_b
             return carry
 
         def level(k, carry):
             press_x, press_y, force_u, force_v, col_u, col_v = carry
-            level_at = lax.convert_element_type(k, F32)
-            act18 = (level_at < code18).astype(F32)
-            act = (level_at < code).astype(F32)
-            bih_u = biharm(k, k, MOVING + k, act18)
-            bih_v = biharm(LEVELS + k, LEVELS + k, MOVING + LEVELS + k, act18)
-            u, v = fx[k, pl.ds(2, ROWS)], fx[LEVELS + k, pl.ds(2, ROWS)]
-            at = 2 * LEVELS + k
-            fx[at, pl.ds(1, 1)] = x_recv[step, 0, pl.ds(2 * MOVING + k, 1)]
-            fx[at, pl.ds(ROWS + 2, 1)] = x_recv[step, 1, pl.ds(2 * MOVING + k, 1)]
-            b = fx[at, pl.ds(2, ROWS)]
-            edge = turn(near, 127 - 2 * at, 1)
-            b_x = fx[at, pl.ds(3, ROWS)] - fx[at, pl.ds(1, ROWS)]
-            b_y = jnp.where(lane == LANES - 1, edge, turn(b, -1, 1)) - jnp.where(
-                lane == 0, edge, turn(b, 1, 1)
-            )
-            dyb[k, pl.ds(0, ROWS)] = b_y
-            press_x, press_y = press_x + b_x, press_y + b_y
+            act = (lax.convert_element_type(k, F32) < code).astype(F32)
+            rows = pl.ds(pl.multiple_of(ROWS * k, ROWS), ROWS)
+            rows_v = pl.ds(pl.multiple_of(ROWS * (LEVELS + k), ROWS), ROWS)
+            bih_u = laplace(k, lp, mom_out[rows])
+            bih_v = laplace(LEVELS + k, lp, mom_out[rows_v])
+            u, v = fx[pl.ds(EXT * k + OWN, ROWS)], fx[pl.ds(EXT * (LEVELS + k) + OWN, ROWS)]
+            at = EXT * (MOVING + k) + OWN
+            press_x = press_x + (fx[pl.ds(at + 1, ROWS)] - fx[pl.ds(at - 1, ROWS)])
+            press_y = press_y + buoy_out[rows, LANES : 2 * LANES]
             tend_u = (-0.25 / LEVELS) * press_x + 0.1 * v - 0.02 * bih_u
             tend_v = (-0.25 / LEVELS) * press_y - 0.1 * u - 0.02 * bih_v
             su = act * (u + 0.2 * tend_u)
@@ -382,10 +456,16 @@
         fy_send[step, 0] = flat_left
         fy_send[step, 1] = flat_right
         start(FORCE, step)
+        rim_laps(buoy_out, MOVING, LEVELS, 2 * MOVING, 2 * MOVING + LEVELS)
+        own_laps(buoy_out, MOVING, LEVELS)
+        stage(buoy_in, MOVING, LEVELS, lp, lap_near)
+        buoy_out[0:rows_b, 0:LANES] = apply(buoy_in, rows_b, LANES)
         lax.fori_loop(0, LEVELS, buoyancy, 0, unroll=True)
         if step < STEPS - 1:
             def pack_b(k, strips):
-                return put_b(step + 1, k, fx[MOVING + k, pl.ds(2, ROWS)], strips)
+                cells = in_3d[2, k]
+                fx[pl.ds(EXT * (MOVING + k) + OWN, ROWS)] = cells
+                return put_b(step + 1, k, cells, strips)
 
             strips = lax.fori_loop(0, LEVELS, pack_b, (zero, zero), unroll=True)
             start(EARLY, step + 1)
@@ -458,14 +538,18 @@
         scratch_shapes=[
             pltpu.VMEM(block, F32),
             pltpu.VMEM(block, F32),
-            pltpu.VMEM((STACK, ext, LANES), F32),
-            pltpu.VMEM((STACK, ext, LANES), F32),
-            pltpu.VMEM((LEVELS, ext, LANES), F32),
+            pltpu.VMEM((STACK * EXT, LANES), F32),
+            pltpu.VMEM((STACK * EXT, LANES), F32),
             pltpu.VMEM((ext, LANES), F32),
             pltpu.VMEM((ext, LANES), F32),
             pltpu.VMEM((FIELDS,) + block, F32),
             pltpu.VMEM((3, ROWS, LANES), F32),
             pltpu.VMEM((2, ROWS, LANES), jnp.int32),
+            pltpu.VMEM((4 * LANES, 2 * LANES), BF16),
+            pltpu.VMEM((MOVING * (ROWS + 2), 4 * LANES), BF16),
+            pltpu.VMEM((LEVELS * (ROWS + 2), 4 * LANES), BF16),
+            pltpu.VMEM((MOVING * (ROWS + 2), LANES), F32),
+            pltpu.VMEM((LEVELS * (ROWS + 2), 2 * LANES), F32),
             pltpu.VMEM((STEPS, 2, RIM, LANES), F32),
             pltpu.VMEM((STEPS, 2, ROWS, LANES), F32),
             pltpu.VMEM((STEPS, 2, RIM, LANES), F32),

time: 31.5 us -> 28.1 us (0.89)
  Pallas kernels: 30.8 us -> 27.4 us
    pallas_call x1, Pallas kernels: 29.9 us -> 26.6 us  [per_device(): pl.pallas_call(kernel, out_shape=outs, in_specs=[hbm] * 8, out_specs=(vme...]
where the time goes in v2:
time: 28.1 us; the launch traced here: 28 us
  Pallas kernels  27.4 us (98%)
  between operations  0.64 us (2%)
    pallas_call x1, Pallas kernels, per_device(): pl.pallas_call(kernel, out_shape=outs, in_specs=[hbm] * 8, out_specs=(vme...  26.6 us
    pallas_call x1, Pallas kernels, per_device(): pl.pallas_call(store_kernel, out_shape=outs, in_specs=[vmem] * 6, out_spe...  0.8 us

profile of v2, /device:TPU:1, one launch (start us, length us, event | category | flops | bytes accessed | tf_op | source)
XLA Modules:
  0.0 28.0 jit_solution(17348941202923721832)
XLA Ops:
  0.6 26.6 %shard_map.127 = (f32[16,16,128]{2,1,0:T(8,128)S(1)}, f32[16,16,128]{2,1,0:T(8,128)S(1)}, f32[16,16,128]{2,1,0:T(8,128)S(1)}, f32[16,128]{1,0:T(8,128)S(1)}, f32...) custom-call(f32[16,16,128]{2,1,0:T(8,128)} %vel_u.1, f32[16,16,128]{2,1,0:T(8,128)} %vel_v.1, f32[16,16,128]{2,1,0:T(8,128)} %buoy.1, ...), custom_call_target="tpu_custom_call" | custom-call | tf_op jit(solution)/shard_map/pallas_call | solution.py:533
  27.2 0.8 %shard_map.128 = (f32[16,16,128]{2,1,0:T(8,128)}, f32[16,16,128]{2,1,0:T(8,128)}, f32[16,16,128]{2,1,0:T(8,128)}, f32[16,128]{1,0:T(8,128)}, f32[16,128]{1,0:T(8,128)}, /*index=5*/f32[16,128]{1,0:T(8,128)}) custom-call(f32[16,16,128]{2,1,0:T(8,128)S(1)} %get-tuple-element.12.refs_0_, f32[16,16,128]{2,1,0:T(8,128)S(1)} %get-tuple-element.13.refs_1_, ...), custom_call_target="tpu_custom_call" | custom-call | tf_op jit(solution)/shard_map/pallas_call | solution.py:574

commit v3 on v2

--- a/solution.py
+++ b/solution.py
@@ -19,14 +19,17 @@
 DIRS = [(-1, 0), (1, 0), (0, -1), (0, 1), (-1, -1), (-1, 1), (1, -1), (1, 1)]
 SIDES = [(-1, -1), (0, -1), (1, -1), (-1, 1), (0, 1), (1, 1)]
 MOVING = 2 * LEVELS
-CODE_ROW = 2 * STACK
-RIM = CODE_ROW + 8
+FLAT_ROW = 2 * MOVING
+BUOY_NEAR = FLAT_ROW + 8
+BUOY_FAR = BUOY_NEAR + LEVELS
+RIM = BUOY_FAR + LEVELS
 HALF = LANES // 2
 
 
 RIMS, FORCE, PLANE, EARLY = 0, 1, 2, 3
 EXT = 32
 OWN = 8
+SCALE = LEVELS / SUB
 
 
 def turn(x, shift, axis):
@@ -84,31 +87,40 @@
     return jnp.concatenate([main, jnp.concatenate(blocks, axis=0)], axis=1)
 
 
-def barotropic(state, push_u, push_v, code_wide):
-    wet = (code_wide > 0.0).astype(F32)
-    depth = code_wide / LEVELS
-    zero = jnp.zeros((ROWS, LANES), F32)
-
-    def substep(_, carry):
+def substep(eta, tu, tv, wet, depth, push=None):
+    div = (turn(tu, -1, 0) - turn(tu, 1, 0)) + (turn(tv, -1, 1) - turn(tv, 1, 1))
+    eta = wet * (eta - 0.125 * div)
+    thick = 0.125 * (depth + eta)
+    new_u = 0.98 * tu - thick * (turn(eta, -1, 0) - turn(eta, 1, 0)) + 0.05 * tv
+    new_v = 0.98 * tv - thick * (turn(eta, -1, 1) - turn(eta, 1, 1)) - 0.05 * tu
+    if push is not None:
+        new_u, new_v = new_u + push[0], new_v + push[1]
+    return eta, wet * new_u, wet * new_v
+
+
+def barotropic(state, push, wet, depth):
+    eta, tu, tv = state
+    tu, tv = tu + wet * push[0], tv + wet * push[1]
+
+    def one(_, carry):
         eta, tu, tv, sum_u, sum_v = carry
-        div = (turn(tu, -1, 0) - turn(tu, 1, 0)) + (turn(tv, -1, 1) - turn(tv, 1, 1))
-        eta = wet * (eta - 0.125 * div)
-        thick = 0.125 * (depth + eta)
-        new_u = wet * (
-            0.98 * tu + push_u - thick * (turn(eta, -1, 0) - turn(eta, 1, 0)) + 0.05 * tv
-        )
-        new_v = wet * (
-            0.98 * tv + push_v - thick * (turn(eta, -1, 1) - turn(eta, 1, 1)) - 0.05 * tu
-        )
-        sum_u = sum_u + new_u[ROWS : 2 * ROWS, 0:LANES]
-        sum_v = sum_v + new_v[ROWS : 2 * ROWS, 0:LANES]
-        return eta, new_u, new_v, sum_u, sum_v
-
-    eta, tu, tv, sum_u, sum_v = lax.fori_loop(
-        0, SUB, substep, state + (zero, zero), unroll=True
+        eta, tu, tv = substep(eta, tu, tv, wet, depth, push)
+        return eta, tu, tv, sum_u + tu, sum_v + tv
+
+    return lax.fori_loop(0, SUB - 1, one, (eta, tu, tv, tu, tv), unroll=True)
+
+
+def inside(cells):
+    return cells[ROWS : 2 * ROWS, 0:LANES]
+
+
+def lane_pair(odd, cells, even_at, odd_at):
+    shape = odd.shape
+    return jnp.where(
+        odd,
+        jnp.broadcast_to(cells[:, odd_at : odd_at + 1], shape),
+        jnp.broadcast_to(cells[:, even_at : even_at + 1], shape),
     )
-    own = tuple(c[ROWS : 2 * ROWS, 0:LANES] for c in (eta, tu, tv))
-    return own, sum_u, sum_v
 
 
 def store_kernel(*refs):
@@ -128,7 +140,7 @@
     vel_u, vel_v, buoy, surface, trans_u, trans_v, ocean, layers,
     out_u, out_v, out_b, out_eta, out_tu, out_tv,
     star_u, star_v,
-    fx, lp, near_ext, code_ext, in_3d, in_2d, in_int,
+    fx, lp, near_ext, ring_rows, rim_new, in_3d, in_2d, in_int,
     lane_w, mom_in, buoy_in, mom_out, buoy_out,
     x_send, y_send, x_recv, y_recv, gx_send, gy_send, gx_recv, gy_recv,
     fx_send, fy_send, fx_recv, fy_recv, in_sem, send_sem, recv_sem,
@@ -197,9 +209,9 @@
                     if step == 0:
                         rows = pl.ds(0, RIM)
                     elif phase == EARLY:
-                        rows = pl.ds(2 * MOVING, 2 * LEVELS)
+                        rows = pl.ds(BUOY_NEAR, 2 * LEVELS)
                     else:
-                        rows = pl.ds(0, 2 * MOVING)
+                        rows = pl.ds(0, BUOY_NEAR)
                     src, dst = x_send.at[step, src_at, rows], x_recv.at[step, dst_at, rows]
             else:
                 src_at, dst_at = (0 if d[1] < 0 else 1), SIDES.index(back)
@@ -207,7 +219,7 @@
                     src, dst = fy_send.at[step, src_at], fy_recv.at[step, dst_at]
                 elif phase == PLANE:
                     src, dst = gy_send.at[step, src_at], gy_recv.at[step, dst_at]
-                elif phase == EARLY:
+                elif step and phase == RIMS:
                     continue
                 else:
                     src, dst = y_send.at[step, src_at], y_recv.at[step, dst_at]
@@ -259,17 +271,16 @@
         return to_left, to_right
 
     def put_v(step, j, cells, strips):
-        fx[pl.ds(EXT * j + OWN, ROWS)] = cells
         return put(step, j, j, MOVING + j, cells, strips)
 
     def put_b(step, k, cells, strips):
         j = MOVING + k
-        return put(step, j, 2 * MOVING + k, 2 * MOVING + LEVELS + k, cells, strips)
-
-    def send_state(step, strips, flats):
-        y_send[step, 0] = strips[0]
-        y_send[step, 1] = strips[1]
-        start(RIMS, step)
+        return put(step, j, BUOY_NEAR + k, BUOY_FAR + k, cells, strips)
+
+    def put_flat(step, a, cells, strips):
+        return put(step, STACK + a, FLAT_ROW + 2 * a, FLAT_ROW + 2 * a + 1, cells, strips)
+
+    def send_plane(step, flats):
         flat_left, flat_right = pack_flat(flats)
         gy_send[step, 0] = flat_left
         gy_send[step, 1] = flat_right
@@ -277,6 +288,7 @@
             gx_send[step, ROWS * a : ROWS * (a + 1)] = cells
         start(PLANE, step)
 
+    ring_rows[...] = jnp.zeros(ring_rows.shape, F32)
     for r, blocks in enumerate(lane_weights()):
         for c, block in enumerate(blocks):
             for at in (2 * r, 2 * r + 1):
@@ -285,52 +297,117 @@
     loads[7].wait()
     lay = in_int[1].astype(F32)
     code = jnp.where(in_int[0] > 0, lay, 0.0)
-    strips = put(0, STACK, CODE_ROW, CODE_ROW + 1, code, (zero, zero))
+    strips = put_flat(0, 0, code, (zero, zero))
     for a in range(FIELDS):
         loads[a].wait()
 
         def pack(k, strips, a=a):
             cells = in_3d[a, k]
+            fx[pl.ds(EXT * (a * LEVELS + k) + OWN, ROWS)] = cells
             if a < 2:
                 return put_v(0, a * LEVELS + k, cells, strips)
-            fx[pl.ds(EXT * (MOVING + k) + OWN, ROWS)] = cells
             return put_b(0, k, cells, strips)
 
         strips = lax.fori_loop(0, LEVELS, pack, strips, unroll=True)
+    flats = [code]
     for a in range(3):
         loads[3 + a].wait()
+        flats.append(in_2d[a])
+        strips = put_flat(0, 1 + a, in_2d[a], strips)
+    y_send[0, 0] = strips[0]
+    y_send[0, 1] = strips[1]
     pl.semaphore_wait(barrier, total_near)
-    sea, flow_u, flow_v = in_2d[0], in_2d[1], in_2d[2]
-    send_state(0, strips, (sea, flow_u, flow_v, code))
+    start(RIMS, 0)
+
+    around = (ROWS + 8, LANES)
+    lane24 = lax.broadcasted_iota(jnp.int32, around, 1)
+    odd24 = (lane24 & 1) == 1
+    level24 = ((lane24 >> 1) & (LEVELS - 1)).astype(F32)
+    level_pair = level24[0:ROWS]
+    moving24 = lane24 < 2 * MOVING
+    is_u24 = lane24 < 2 * LEVELS
+    upper = lax.broadcasted_iota(jnp.int32, (8, LANES), 0) < 4
+
+    def cyclic(own, below, above):
+        return jnp.concatenate([own, jnp.where(upper, below, above)], axis=0)
+
+    def beside_columns(left24, right24, j):
+        return jnp.where(
+            lane24 < HALF, turn(right24, -2 * j - 2, 1), turn(left24, 126 - 2 * j, 1)
+        )
+
+    def side24(cells):
+        tile = cells[:, LANES : 2 * LANES]
+        return cyclic(tile[ROWS : 2 * ROWS], tile[2 * ROWS : 2 * ROWS + 8], tile[8:ROWS])
 
     for step in range(STEPS):
-        arrive(RIMS, step)
-        if step:
+        if step == 0:
+            arrive(RIMS, step)
+        else:
+            arrive(RIMS, step)
             arrive(EARLY, step)
-        from_left, from_right = y_recv[step, 1], y_recv[step, 4]
-        near = jnp.where(odd, from_left, turn(from_right, -2, 1))
-        far = jnp.where(odd, turn(from_left, 1, 1), turn(from_right, -3, 1))
+        left24 = cyclic(y_recv[step, 1], y_recv[step, 2, 0:8], y_recv[step, 0, 8:16])
+        right24 = cyclic(y_recv[step, 4], y_recv[step, 5, 0:8], y_recv[step, 3, 8:16])
+        near24 = jnp.where(odd24, left24, turn(right24, -2, 1))
+        far = jnp.where(odd, turn(left24[0:ROWS], 1, 1), turn(right24[0:ROWS], -3, 1))
         inner = turn(jnp.where(odd, strips[1], strips[0]), -1, 1)
-        near_ext[pl.ds(1, ROWS)] = near
-        odd8 = odd[0:8]
-        top = jnp.where(odd8, y_recv[step, 0, 8:16], turn(y_recv[step, 3, 8:16], -2, 1))
-        low = jnp.where(odd8, y_recv[step, 2, 0:8], turn(y_recv[step, 5, 0:8], -2, 1))
-        near_ext[pl.ds(0, 1)] = top[7:8]
-        near_ext[pl.ds(ROWS + 1, 1)] = low[0:1]
 
         if step == 0:
-            code_ext[pl.ds(0, 1)] = x_recv[0, 0, pl.ds(CODE_ROW, 1)]
-            code_ext[pl.ds(ROWS + 1, 1)] = x_recv[0, 1, pl.ds(CODE_ROW, 1)]
-            at = 2 * STACK
-            code_near = jnp.where(
-                odd,
-                jnp.broadcast_to(near[:, at + 1 : at + 2], (ROWS, LANES)),
-                jnp.broadcast_to(near[:, at : at + 1], (ROWS, LANES)),
+            code_near = lane_pair(odd24, near24, 2 * STACK, 2 * STACK + 1)
+            code_far = lane_pair(odd, far, 2 * STACK, 2 * STACK + 1)
+            code_inner = lane_pair(odd, code, LANES - 1, 0)
+            act_near = level24 < code_near
+        else:
+            shift_side = [
+                (SCALE * side24(total) - beside_columns(left24, right24, STACK + 1 + a))
+                / jnp.maximum(code_side, 1.0)
+                for a, total in enumerate((sum_u, sum_v))
+            ]
+
+            def couple_pairs(cells, near_code, rows, levels, even_at, odd_at, sources):
+                parity = odd24[0:rows]
+                shift = jnp.where(
+                    is_u24[0:rows],
+                    lane_pair(parity, sources[0][0:rows], even_at, odd_at),
+                    lane_pair(parity, sources[1][0:rows], even_at, odd_at),
+                )
+                moved = jnp.where(levels < near_code, cells + shift, 0.0)
+                return jnp.where(moving24[0:rows], moved, cells)
+
+            near24 = couple_pairs(
+                near24, code_near, ROWS + 8, level24, 0, LANES - 1, shift_side
             )
-            act_near = ((pair & (LEVELS - 1)).astype(F32) < code_near).astype(F32)
-        lap_near = act_near * (
-            far + inner + near_ext[pl.ds(0, ROWS)] + near_ext[pl.ds(2, ROWS)] - 4.0 * near
-        )
+            far = couple_pairs(far, code_far, ROWS, level_pair, 1, LANES - 2, shift_side)
+            inner = couple_pairs(
+                inner, code_inner, ROWS, level_pair, LANES - 1, 0, (shift_u, shift_v)
+            )
+            level16 = lax.broadcasted_iota(jnp.int32, (LEVELS, LANES), 0).astype(F32)
+            for side in range(2):
+                for away in range(2):
+                    at = (ROWS - 1 - away, 2 * ROWS + away)[side]
+                    code_row = x_recv[0, side, pl.ds(FLAT_ROW + away, 1)]
+                    for a, total in enumerate((sum_u, sum_v)):
+                        column = x_recv[1, side, pl.ds(FLAT_ROW + 2 * (1 + a) + away, 1)]
+                        shift = (
+                            SCALE * total[at : at + 1, 0:LANES] - column
+                        ) / jnp.maximum(code_row, 1.0)
+                        rows = pl.ds(MOVING * away + LEVELS * a, LEVELS)
+                        rim_new[side, rows] = jnp.where(
+                            level16 < code_row, x_recv[1, side, rows] + shift, 0.0
+                        )
+
+        near_ext[...] = near24
+        near = near24[0:ROWS]
+        lap_near = jnp.where(
+            act_near,
+            turn(near24, 1, 0) + turn(near24, -1, 0) - 4.0 * near24,
+            0.0,
+        )[0:ROWS] + jnp.where(act_near[0:ROWS], far + inner, 0.0)
+
+        def rim_cells(side, first, count, at):
+            if first == 0 and step:
+                return rim_new[side, pl.ds(at, count)]
+            return x_recv[step, side, pl.ds(at, count)]
 
         def put_parts(ref, at, rows, parts, col):
             for c, part in enumerate(parts):
@@ -350,10 +427,10 @@
             row = lax.broadcasted_iota(jnp.int32, (count, LANES), 0)
             group = lax.broadcasted_iota(jnp.int32, (count, LANES), 1) >> 1
             for side in range(2):
-                cells = x_recv[step, side, pl.ds(near_at, count)]
+                cells = rim_cells(side, first, count, near_at)
                 at = ROWS * count + count * side
                 corner = jnp.broadcast_to(
-                    near_ext[pl.ds((ROWS + 1) * side, 1)], (count, LANES)
+                    near_ext[pl.ds((ROWS + 7, ROWS)[side], 1)], (count, LANES)
                 )
                 put_parts(ref, at, count, split(cells), 0)
                 put_parts(ref, at, count, pick(group == first + row, corner), 2)
@@ -362,12 +439,13 @@
         def rim_laps(ref, first, count, near_at, far_at):
             level_of = lax.broadcasted_iota(jnp.int32, (count, LANES), 0) & (LEVELS - 1)
             for side in range(2):
-                cells = x_recv[step, side, pl.ds(near_at, count)]
-                beside = x_recv[step, side, pl.ds(far_at, count)] + x_send[
-                    step, side, pl.ds(near_at, count)
+                cells = rim_cells(side, first, count, near_at)
+                edge = EXT * first + (OWN, OWN + ROWS - 1)[side]
+                beside = rim_cells(side, first, count, far_at) + fx[
+                    pl.ds(edge, count, stride=EXT)
                 ]
                 lanes_sum = ref[pl.ds(ROWS * count + count * side, count), 0:LANES]
-                code_row = code_ext[pl.ds((ROWS + 1) * side, 1)]
+                code_row = x_recv[0, side, pl.ds(FLAT_ROW, 1)]
                 lap = jnp.where(
                     level_of.astype(F32) < code_row, beside + lanes_sum - 4.0 * cells, 0.0
                 )
@@ -396,9 +474,30 @@
             )
 
         rows_uv, rows_b = MOVING * ROWS, LEVELS * ROWS
-        rim_rows(buoy_in, MOVING, LEVELS, 2 * MOVING)
+        rim_rows(buoy_in, MOVING, LEVELS, BUOY_NEAR)
         stage(buoy_in, MOVING, LEVELS, fx, near)
         buoy_out[...] = apply(buoy_in, rows_b + 2 * LEVELS, 2 * LANES)
+        if step == 0:
+            grids = []
+            for a, own in enumerate(flats):
+                near_at, far_at = FLAT_ROW + 2 * a, FLAT_ROW + 2 * a + 1
+                ring_rows[a, 0:1] = x_recv[0, 1, pl.ds(near_at, 1)]
+                ring_rows[a, 1:2] = x_recv[0, 1, pl.ds(far_at, 1)]
+                ring_rows[a, 6:7] = x_recv[0, 0, pl.ds(far_at, 1)]
+                ring_rows[a, 7:8] = x_recv[0, 0, pl.ds(near_at, 1)]
+                main = jnp.concatenate([own, ring_rows[a]], axis=0)
+                grids.append(jnp.concatenate(
+                    [main, beside_columns(left24, right24, STACK + a)], axis=1
+                ))
+            code_side = grids[0][:, LANES : 2 * LANES]
+            ahead = substep(
+                *grids[1:], (grids[0] > 0.0).astype(F32), grids[0] / LEVELS
+            )
+            flats = [cells[0:ROWS, 0:LANES] for cells in ahead]
+            send_plane(step, flats + [code])
+        else:
+            flats = [inside(c) for c in substep(eta, flow_u, flow_v, wet, depth)]
+            send_plane(step, flats)
         rim_rows(mom_in, 0, MOVING, 0)
         stage(mom_in, 0, MOVING, fx, near)
         mom_out[...] = apply(mom_in, rows_uv + 2 * MOVING, LANES)
@@ -456,7 +555,16 @@
         fy_send[step, 0] = flat_left
         fy_send[step, 1] = flat_right
         start(FORCE, step)
-        rim_laps(buoy_out, MOVING, LEVELS, 2 * MOVING, 2 * MOVING + LEVELS)
+        if step < STEPS - 1:
+            def pack_star(k, strips):
+                strips = put_v(step + 1, k, star_u[k], strips)
+                return put_v(step + 1, LEVELS + k, star_v[k], strips)
+
+            strips = lax.fori_loop(0, LEVELS, pack_star, (zero, zero), unroll=True)
+            strips = put_flat(step + 1, 1, col_u, strips)
+            strips = put_flat(step + 1, 2, col_v, strips)
+            start(RIMS, step + 1)
+        rim_laps(buoy_out, MOVING, LEVELS, BUOY_NEAR, BUOY_FAR)
         own_laps(buoy_out, MOVING, LEVELS)
         stage(buoy_in, MOVING, LEVELS, lp, lap_near)
         buoy_out[0:rows_b, 0:LANES] = apply(buoy_in, rows_b, LANES)
@@ -467,7 +575,9 @@
                 fx[pl.ds(EXT * (MOVING + k) + OWN, ROWS)] = cells
                 return put_b(step + 1, k, cells, strips)
 
-            strips = lax.fori_loop(0, LEVELS, pack_b, (zero, zero), unroll=True)
+            strips = lax.fori_loop(0, LEVELS, pack_b, strips, unroll=True)
+            y_send[step + 1, 0] = strips[0]
+            y_send[step + 1, 1] = strips[1]
             start(EARLY, step + 1)
         arrive(PLANE, step)
         sides = [gy_recv[step, r] for r in range(6)]
@@ -478,40 +588,38 @@
 
         if step == 0:
             code_wide = plane(code, 3)
-        state = (plane(sea, 0), plane(flow_u, 1), plane(flow_v, 2))
+            wet, depth = (code_wide > 0.0).astype(F32), code_wide / LEVELS
+        state = [plane(cells, a) for a, cells in enumerate(flats)]
         arrive(FORCE, step)
         sides_f = [fy_recv[step, r] for r in range(6)]
-        push_u, push_v = (
+        push = [
             0.2 * wide(
                 own, fx_recv[step, 0, ROWS * a : ROWS * (a + 1)],
                 fx_recv[step, 1, ROWS * a : ROWS * (a + 1)], sides_f, a,
             )
             for a, own in enumerate((force_u, force_v))
-        )
-        (sea, flow_u, flow_v), sum_u, sum_v = barotropic(state, push_u, push_v, code_wide)
-        scale = LEVELS / SUB
-        shift_u = (scale * sum_u - col_u) / lay
-        shift_v = (scale * sum_v - col_v) / lay
-        if step < STEPS - 1:
-            def couple(k, strips):
-                act = (lax.convert_element_type(k, F32) < code).astype(F32)
-                strips = put_v(step + 1, k, act * (star_u[k] + shift_u), strips)
-                return put_v(step + 1, LEVELS + k, act * (star_v[k] + shift_v), strips)
-
-            strips = lax.fori_loop(0, LEVELS, couple, strips, unroll=True)
-            send_state(step + 1, strips, (sea, flow_u, flow_v))
-        else:
-            def finish(k, carry):
-                act = lax.convert_element_type(k, F32) < code
-                out_u[k] = jnp.where(act, star_u[k] + shift_u, 0.0)
-                out_v[k] = jnp.where(act, star_v[k] + shift_v, 0.0)
-                return carry
-
-            lax.fori_loop(0, LEVELS, finish, 0, unroll=True)
-            out_eta[...] = sea
-            out_tu[...] = flow_u
-            out_tv[...] = flow_v
-
+        ]
+        eta, flow_u, flow_v, sum_u, sum_v = barotropic(state, push, wet, depth)
+        shift_u = (SCALE * inside(sum_u) - col_u) / lay
+        shift_v = (SCALE * inside(sum_v) - col_v) / lay
+
+        def couple(k, carry):
+            act = lax.convert_element_type(k, F32) < code
+            new_u = jnp.where(act, star_u[k] + shift_u, 0.0)
+            new_v = jnp.where(act, star_v[k] + shift_v, 0.0)
+            if step == STEPS - 1:
+                out_u[k] = new_u
+                out_v[k] = new_v
+            else:
+                fx[pl.ds(EXT * k + OWN, ROWS)] = new_u
+                fx[pl.ds(EXT * (LEVELS + k) + OWN, ROWS)] = new_v
+            return carry
+
+        lax.fori_loop(0, LEVELS, couple, 0, unroll=True)
+
+    out_eta[...] = inside(eta)
+    out_tu[...] = inside(flow_u)
+    out_tv[...] = inside(flow_v)
     for step in range(STEPS):
         for phase in (RIMS, FORCE, PLANE, EARLY):
             if phase != EARLY or step:
@@ -528,7 +636,6 @@
         pltpu.with_memory_space_constraint(x, pltpu.HBM)
         for x in (velocity_u, velocity_v, buoyancy, surface, transport_u, transport_v, ocean, layers)
     ]
-    ext = 24
     block = (LEVELS, ROWS, LANES)
     middle = pl.pallas_call(
         kernel,
@@ -540,8 +647,9 @@
             pltpu.VMEM(block, F32),
             pltpu.VMEM((STACK * EXT, LANES), F32),
             pltpu.VMEM((STACK * EXT, LANES), F32),
-            pltpu.VMEM((ext, LANES), F32),
-            pltpu.VMEM((ext, LANES), F32),
+            pltpu.VMEM((ROWS + 8, LANES), F32),
+            pltpu.VMEM((4, 8, LANES), F32),
+            pltpu.VMEM((2, 2 * MOVING, LANES), F32),
             pltpu.VMEM((FIELDS,) + block, F32),
             pltpu.VMEM((3, ROWS, LANES), F32),
             pltpu.VMEM((2, ROWS, LANES), jnp.int32),

time: 28.1 us -> 25.2 us (0.90)
  Pallas kernels: 27.4 us -> 24.4 us
    pallas_call x1, Pallas kernels: 26.6 us -> 23.6 us  [per_device(): pl.pallas_call(kernel, out_shape=outs, in_specs=[hbm] * 8, out_specs=(vme...]
where the time goes in v3:
time: 25.2 us; the launch traced here: 25 us
  Pallas kernels  24.4 us (97%)
  between operations  0.64 us (3%)
    pallas_call x1, Pallas kernels, per_device(): pl.pallas_call(kernel, out_shape=outs, in_specs=[hbm] * 8, out_specs=(vme...  23.6 us
    pallas_call x1, Pallas kernels, per_device(): pl.pallas_call(store_kernel, out_shape=outs, in_specs=[vmem] * 6, out_spe...  0.8 us

profile of v3, /device:TPU:1, one launch (start us, length us, event | category | flops | bytes accessed | tf_op | source)
XLA Modules:
  0.0 25.0 jit_solution(15111967934159675153)
XLA Ops:
  0.6 23.6 %shard_map.127 = (f32[16,16,128]{2,1,0:T(8,128)S(1)}, f32[16,16,128]{2,1,0:T(8,128)S(1)}, f32[16,16,128]{2,1,0:T(8,128)S(1)}, f32[16,128]{1,0:T(8,128)S(1)}, f32...) custom-call(f32[16,16,128]{2,1,0:T(8,128)} %vel_u.1, f32[16,16,128]{2,1,0:T(8,128)} %vel_v.1, f32[16,16,128]{2,1,0:T(8,128)} %buoy.1, ...), custom_call_target="tpu_custom_call" | custom-call | tf_op jit(solution)/shard_map/pallas_call | solution.py:640
  24.2 0.8 %shard_map.128 = (f32[16,16,128]{2,1,0:T(8,128)}, f32[16,16,128]{2,1,0:T(8,128)}, f32[16,16,128]{2,1,0:T(8,128)}, f32[16,128]{1,0:T(8,128)}, f32[16,128]{1,0:T(8,128)}, /*index=5*/f32[16,128]{1,0:T(8,128)}) custom-call(f32[16,16,128]{2,1,0:T(8,128)S(1)} %get-tuple-element.12.refs_0_, f32[16,16,128]{2,1,0:T(8,128)S(1)} %get-tuple-element.13.refs_1_, ...), custom_call_target="tpu_custom_call" | custom-call | tf_op jit(solution)/shard_map/pallas_call | solution.py:682

commit v4 on v3

--- a/solution.py
+++ b/solution.py
@@ -1,3 +1,5 @@
+import functools
+
 import jax
 import jax.numpy as jnp
 from jax import lax
@@ -227,32 +229,51 @@
                         rows = pl.ds(0, 8) if d[0] < 0 else pl.ds(8, 8)
                         src, dst = src.at[rows], dst.at[rows]
             at = phase * STEPS + step
-            copy = pltpu.make_async_remote_copy(
-                src_ref=src, dst_ref=dst,
+            copy = functools.partial(
+                pltpu.make_async_remote_copy, src_ref=src, dst_ref=dst,
                 send_sem=send_sem.at[at, i], recv_sem=recv_sem.at[at, DIRS.index(back)],
                 device_id=(gx + d[0], gy + d[1]), device_id_type=MESH,
             )
             result.append((d, copy))
         return result
 
+    odd_row = lax.rem(gx, 2) == 1
+
+    def start_rows(phase, step, two_hops):
+        pending = [(d, copy) for d, copy in copies(phase, step) if d[0]]
+        pending.sort(key=lambda item: (item[0][1] == 0) != two_hops)
+        for d, copy in pending:
+            @pl.when(jnp.logical_and(here[d], odd_row == (two_hops == (d[0] > 0))))
+            def _(copy=copy):
+                copy().start()
+
+    def start_far(phase, step):
+        start_rows(phase, step, True)
+        for d, copy in copies(phase, step):
+            if d[0] == 0:
+                @pl.when(here[d])
+                def _(copy=copy):
+                    copy().start()
+
+    def start_near(phase, step):
+        start_rows(phase, step, False)
+
     def start(phase, step):
-        for d, copy in copies(phase, step):
-            @pl.when(here[d])
-            def _(copy=copy):
-                copy.start()
+        start_far(phase, step)
+        start_near(phase, step)
 
     def arrive(phase, step):
         by_dir = dict(copies(phase, step))
         for d in by_dir:
             @pl.when(here[d])
             def _(d=d):
-                by_dir[(-d[0], -d[1])].wait_recv()
+                by_dir[(-d[0], -d[1])]().wait_recv()
 
     def sent(phase, step):
         for d, copy in copies(phase, step):
             @pl.when(here[d])
             def _(copy=copy):
-                copy.wait_send()
+                copy().wait_send()
 
     lane = lax.broadcasted_iota(jnp.int32, (ROWS, LANES), 1)
     pair = lane >> 1
@@ -293,6 +314,26 @@
         for c, block in enumerate(blocks):
             for at in (2 * r, 2 * r + 1):
                 lane_w[LANES * at : LANES * (at + 1), LANES * c : LANES * (c + 1)] = block
+    def put_parts(ref, at, rows, parts, col):
+        for c, part in enumerate(parts):
+            ref[pl.ds(at, rows), LANES * (col + c) : LANES * (col + c + 1)] = part
+
+    def stage_own(ref, first, count, source):
+        def one(i, carry):
+            at = pl.multiple_of(ROWS * i, ROWS)
+            put_parts(ref, at, ROWS, split(source[pl.ds(EXT * (first + i) + OWN, ROWS)]), 0)
+            return carry
+
+        lax.fori_loop(0, count, one, 0, unroll=True)
+
+    def stage_edge(ref, first, count, edge):
+        def one(i, carry):
+            at = pl.multiple_of(ROWS * i, ROWS)
+            put_parts(ref, at, ROWS, pick(pair == first + i, edge), 2)
+            return carry
+
+        lax.fori_loop(0, count, one, 0, unroll=True)
+
     loads[6].wait()
     loads[7].wait()
     lay = in_int[1].astype(F32)
@@ -317,7 +358,10 @@
     y_send[0, 0] = strips[0]
     y_send[0, 1] = strips[1]
     pl.semaphore_wait(barrier, total_near)
-    start(RIMS, 0)
+    start_far(RIMS, 0)
+    stage_own(mom_in, 0, MOVING, fx)
+    start_near(RIMS, 0)
+    stage_own(buoy_in, MOVING, LEVELS, fx)
 
     around = (ROWS + 8, LANES)
     lane24 = lax.broadcasted_iota(jnp.int32, around, 1)
@@ -409,20 +453,6 @@
                 return rim_new[side, pl.ds(at, count)]
             return x_recv[step, side, pl.ds(at, count)]
 
-        def put_parts(ref, at, rows, parts, col):
-            for c, part in enumerate(parts):
-                ref[pl.ds(at, rows), LANES * (col + c) : LANES * (col + c + 1)] = part
-
-        def stage(ref, first, count, source, edge):
-            def one(i, carry):
-                at = pl.multiple_of(ROWS * i, ROWS)
-                cells = source[pl.ds(EXT * (first + i) + OWN, ROWS)]
-                put_parts(ref, at, ROWS, split(cells), 0)
-                put_parts(ref, at, ROWS, pick(pair == first + i, edge), 2)
-                return carry
-
-            lax.fori_loop(0, count, one, 0, unroll=True)
-
         def rim_rows(ref, first, count, near_at):
             row = lax.broadcasted_iota(jnp.int32, (count, LANES), 0)
             group = lax.broadcasted_iota(jnp.int32, (count, LANES), 1) >> 1
@@ -475,7 +505,7 @@
 
         rows_uv, rows_b = MOVING * ROWS, LEVELS * ROWS
         rim_rows(buoy_in, MOVING, LEVELS, BUOY_NEAR)
-        stage(buoy_in, MOVING, LEVELS, fx, near)
+        stage_edge(buoy_in, MOVING, LEVELS, near)
         buoy_out[...] = apply(buoy_in, rows_b + 2 * LEVELS, 2 * LANES)
         if step == 0:
             grids = []
@@ -499,11 +529,12 @@
             flats = [inside(c) for c in substep(eta, flow_u, flow_v, wet, depth)]
             send_plane(step, flats)
         rim_rows(mom_in, 0, MOVING, 0)
-        stage(mom_in, 0, MOVING, fx, near)
+        stage_edge(mom_in, 0, MOVING, near)
         mom_out[...] = apply(mom_in, rows_uv + 2 * MOVING, LANES)
         rim_laps(mom_out, 0, MOVING, 0, MOVING)
         own_laps(mom_out, 0, MOVING)
-        stage(mom_in, 0, MOVING, lp, lap_near)
+        stage_own(mom_in, 0, MOVING, lp)
+        stage_edge(mom_in, 0, MOVING, lap_near)
         mom_out[0:rows_uv] = apply(mom_in, rows_uv, LANES)
 
         def buoyancy(k, carry):
@@ -563,10 +594,11 @@
             strips = lax.fori_loop(0, LEVELS, pack_star, (zero, zero), unroll=True)
             strips = put_flat(step + 1, 1, col_u, strips)
             strips = put_flat(step + 1, 2, col_v, strips)
-            start(RIMS, step + 1)
+            start_far(RIMS, step + 1)
         rim_laps(buoy_out, MOVING, LEVELS, BUOY_NEAR, BUOY_FAR)
         own_laps(buoy_out, MOVING, LEVELS)
-        stage(buoy_in, MOVING, LEVELS, lp, lap_near)
+        stage_own(buoy_in, MOVING, LEVELS, lp)
+        stage_edge(buoy_in, MOVING, LEVELS, lap_near)
         buoy_out[0:rows_b, 0:LANES] = apply(buoy_in, rows_b, LANES)
         lax.fori_loop(0, LEVELS, buoyancy, 0, unroll=True)
         if step < STEPS - 1:
@@ -578,7 +610,10 @@
             strips = lax.fori_loop(0, LEVELS, pack_b, strips, unroll=True)
             y_send[step + 1, 0] = strips[0]
             y_send[step + 1, 1] = strips[1]
-            start(EARLY, step + 1)
+            start_far(EARLY, step + 1)
+            start_near(RIMS, step + 1)
+            start_near(EARLY, step + 1)
+            stage_own(buoy_in, MOVING, LEVELS, fx)
         arrive(PLANE, step)
         sides = [gy_recv[step, r] for r in range(6)]
 
@@ -616,6 +651,8 @@
             return carry
 
         lax.fori_loop(0, LEVELS, couple, 0, unroll=True)
+        if step < STEPS - 1:
+            stage_own(mom_in, 0, MOVING, fx)
 
     out_eta[...] = inside(eta)
     out_tu[...] = inside(flow_u)

time: 25.2 us -> 24.1 us (0.956)
  Pallas kernels: 24.4 us -> 23.3 us
    pallas_call x1, Pallas kernels: 23.6 us -> 22.5 us  [per_device(): pl.pallas_call(kernel, out_shape=outs, in_specs=[hbm] * 8, out_specs=(vme...]
where the time goes in v4:
time: 24.1 us; the launch traced here: 23.9 us
  Pallas kernels  23.3 us (97%)
  between operations  0.64 us (3%)
    pallas_call x1, Pallas kernels, per_device(): pl.pallas_call(kernel, out_shape=outs, in_specs=[hbm] * 8, out_specs=(vme...  22.5 us
    pallas_call x1, Pallas kernels, per_device(): pl.pallas_call(store_kernel, out_shape=outs, in_specs=[vmem] * 6, out_spe...  0.8 us

profile of v4, /device:TPU:1, one launch (start us, length us, event | category | flops | bytes accessed | tf_op | source)
XLA Modules:
  0.0 23.9 jit_solution(11239644335391837525)
XLA Ops:
  0.6 22.5 %shard_map.127 = (f32[16,16,128]{2,1,0:T(8,128)S(1)}, f32[16,16,128]{2,1,0:T(8,128)S(1)}, f32[16,16,128]{2,1,0:T(8,128)S(1)}, f32[16,128]{1,0:T(8,128)S(1)}, f32...) custom-call(f32[16,16,128]{2,1,0:T(8,128)} %vel_u.1, f32[16,16,128]{2,1,0:T(8,128)} %vel_v.1, f32[16,16,128]{2,1,0:T(8,128)} %buoy.1, ...), custom_call_target="tpu_custom_call" | custom-call | tf_op jit(solution)/shard_map/pallas_call | solution.py:677
  23.1 0.8 %shard_map.128 = (f32[16,16,128]{2,1,0:T(8,128)}, f32[16,16,128]{2,1,0:T(8,128)}, f32[16,16,128]{2,1,0:T(8,128)}, f32[16,128]{1,0:T(8,128)}, f32[16,128]{1,0:T(8,128)}, /*index=5*/f32[16,128]{1,0:T(8,128)}) custom-call(f32[16,16,128]{2,1,0:T(8,128)S(1)} %get-tuple-element.12.refs_0_, f32[16,16,128]{2,1,0:T(8,128)S(1)} %get-tuple-element.13.refs_1_, ...), custom_call_target="tpu_custom_call" | custom-call | tf_op jit(solution)/shard_map/pallas_call | solution.py:719

commit v5 on v4

--- a/solution.py
+++ b/solution.py
@@ -24,7 +24,8 @@
 FLAT_ROW = 2 * MOVING
 BUOY_NEAR = FLAT_ROW + 8
 BUOY_FAR = BUOY_NEAR + LEVELS
-RIM = BUOY_FAR + LEVELS
+CODE_PLANE = BUOY_FAR + LEVELS
+RIM = CODE_PLANE + ROWS
 HALF = LANES // 2
 
 
@@ -205,11 +206,10 @@
                 if phase == FORCE:
                     src, dst = fx_send.at[step], fx_recv.at[step, dst_at]
                 elif phase == PLANE:
-                    rows = pl.ds(0, (4 if step == 0 else 3) * ROWS)
-                    src, dst = gx_send.at[step, rows], gx_recv.at[step, dst_at, rows]
+                    src, dst = gx_send.at[step], gx_recv.at[step, dst_at]
                 else:
                     if step == 0:
-                        rows = pl.ds(0, RIM)
+                        rows = pl.ds(0, BUOY_FAR) if phase == RIMS else pl.ds(BUOY_FAR, RIM - BUOY_FAR)
                     elif phase == EARLY:
                         rows = pl.ds(BUOY_NEAR, 2 * LEVELS)
                     else:
@@ -218,10 +218,10 @@
             else:
                 src_at, dst_at = (0 if d[1] < 0 else 1), SIDES.index(back)
                 if phase == FORCE:
-                    src, dst = fy_send.at[step, src_at], fy_recv.at[step, dst_at]
+                    src, dst = fy_send.at[step], fy_recv.at[step, dst_at]
                 elif phase == PLANE:
                     src, dst = gy_send.at[step, src_at], gy_recv.at[step, dst_at]
-                elif step and phase == RIMS:
+                elif phase == (RIMS if step else EARLY):
                     continue
                 else:
                     src, dst = y_send.at[step, src_at], y_recv.at[step, dst_at]
@@ -277,7 +277,9 @@
 
     lane = lax.broadcasted_iota(jnp.int32, (ROWS, LANES), 1)
     pair = lane >> 1
+    lane8 = lane[0:8]
     odd = (lane & 1) == 1
+    rim_lanes = jnp.logical_or(lane < 16, lane >= LANES - 16)
     zero = jnp.zeros((ROWS, LANES), F32)
 
     def put(step, j, near_at, far_at, cells, strips):
@@ -305,7 +307,7 @@
         flat_left, flat_right = pack_flat(flats)
         gy_send[step, 0] = flat_left
         gy_send[step, 1] = flat_right
-        for a, cells in enumerate(flats):
+        for a, cells in enumerate(flats[0:3]):
             gx_send[step, ROWS * a : ROWS * (a + 1)] = cells
         start(PLANE, step)
 
@@ -355,12 +357,16 @@
         loads[3 + a].wait()
         flats.append(in_2d[a])
         strips = put_flat(0, 1 + a, in_2d[a], strips)
+    strips = turn(strips[0], -2, 1), strips[1]
     y_send[0, 0] = strips[0]
     y_send[0, 1] = strips[1]
     pl.semaphore_wait(barrier, total_near)
+    for side in range(2):
+        x_send[0, side, pl.ds(CODE_PLANE, ROWS)] = code
     start_far(RIMS, 0)
     stage_own(mom_in, 0, MOVING, fx)
     start_near(RIMS, 0)
+    start(EARLY, 0)
     stage_own(buoy_in, MOVING, LEVELS, fx)
 
     around = (ROWS + 8, LANES)
@@ -377,7 +383,7 @@
 
     def beside_columns(left24, right24, j):
         return jnp.where(
-            lane24 < HALF, turn(right24, -2 * j - 2, 1), turn(left24, 126 - 2 * j, 1)
+            lane24 < HALF, turn(right24, -2 * j, 1), turn(left24, 126 - 2 * j, 1)
         )
 
     def side24(cells):
@@ -392,9 +398,10 @@
             arrive(EARLY, step)
         left24 = cyclic(y_recv[step, 1], y_recv[step, 2, 0:8], y_recv[step, 0, 8:16])
         right24 = cyclic(y_recv[step, 4], y_recv[step, 5, 0:8], y_recv[step, 3, 8:16])
-        near24 = jnp.where(odd24, left24, turn(right24, -2, 1))
-        far = jnp.where(odd, turn(left24[0:ROWS], 1, 1), turn(right24[0:ROWS], -3, 1))
-        inner = turn(jnp.where(odd, strips[1], strips[0]), -1, 1)
+        near24 = jnp.where(odd24, left24, right24)
+        far = jnp.where(odd, right24[0:ROWS], left24[0:ROWS])
+        far = jnp.where(odd, turn(far, 1, 1), turn(far, -1, 1))
+        inner = jnp.where(odd, turn(strips[0], 1, 1), turn(strips[1], -1, 1))
 
         if step == 0:
             code_near = lane_pair(odd24, near24, 2 * STACK, 2 * STACK + 1)
@@ -582,9 +589,13 @@
         force_u, force_v = force_u / LEVELS, force_v / LEVELS
         fx_send[step, 0:ROWS] = force_u
         fx_send[step, ROWS : 2 * ROWS] = force_v
-        flat_left, flat_right = pack_flat((force_u, force_v))
-        fy_send[step, 0] = flat_left
-        fy_send[step, 1] = flat_right
+        fy_send[step] = jnp.where(
+            rim_lanes[0:8], force_u[0:8],
+            jnp.where(
+                lane8 < 48, turn(force_u[8:16], 32, 1),
+                jnp.where(lane8 < 80, turn(force_v[0:8], 64, 1), turn(force_v[8:16], 96, 1)),
+            ),
+        )
         start(FORCE, step)
         if step < STEPS - 1:
             def pack_star(k, strips):
@@ -595,6 +606,8 @@
             strips = put_flat(step + 1, 1, col_u, strips)
             strips = put_flat(step + 1, 2, col_v, strips)
             start_far(RIMS, step + 1)
+        if step == 0:
+            arrive(EARLY, step)
         rim_laps(buoy_out, MOVING, LEVELS, BUOY_NEAR, BUOY_FAR)
         own_laps(buoy_out, MOVING, LEVELS)
         stage_own(buoy_in, MOVING, LEVELS, lp)
@@ -608,6 +621,7 @@
                 return put_b(step + 1, k, cells, strips)
 
             strips = lax.fori_loop(0, LEVELS, pack_b, strips, unroll=True)
+            strips = turn(strips[0], -2, 1), strips[1]
             y_send[step + 1, 0] = strips[0]
             y_send[step + 1, 1] = strips[1]
             start_far(EARLY, step + 1)
@@ -622,18 +636,24 @@
             return wide(own, gx_recv[step, 0, rows], gx_recv[step, 1, rows], sides, a)
 
         if step == 0:
-            code_wide = plane(code, 3)
+            rows = pl.ds(CODE_PLANE, ROWS)
+            code_wide = wide(code, x_recv[0, 0, rows], x_recv[0, 1, rows], sides, 3)
             wet, depth = (code_wide > 0.0).astype(F32), code_wide / LEVELS
         state = [plane(cells, a) for a, cells in enumerate(flats)]
         arrive(FORCE, step)
-        sides_f = [fy_recv[step, r] for r in range(6)]
-        push = [
-            0.2 * wide(
-                own, fx_recv[step, 0, ROWS * a : ROWS * (a + 1)],
-                fx_recv[step, 1, ROWS * a : ROWS * (a + 1)], sides_f, a,
-            )
-            for a, own in enumerate((force_u, force_v))
-        ]
+        beside = [[], []]
+        for r in range(3):
+            strip = jnp.where((lane8 & 16) == 0, fy_recv[step, r + 3], fy_recv[step, r])
+            for part in range(4):
+                rolled = turn(strip, -32 * part, 1) if part else strip
+                beside[part // 2].append(jnp.where(rim_lanes[0:8], rolled, 0.0))
+        push = []
+        for a, own in enumerate((force_u, force_v)):
+            rows = slice(ROWS * a, ROWS * (a + 1))
+            main = [fx_recv[step, 0, rows], own, fx_recv[step, 1, rows]]
+            push.append(0.2 * jnp.concatenate(
+                [jnp.concatenate(main, axis=0), jnp.concatenate(beside[a], axis=0)], axis=1
+            ))
         eta, flow_u, flow_v, sum_u, sum_v = barotropic(state, push, wet, depth)
         shift_u = (SCALE * inside(sum_u) - col_u) / lay
         shift_v = (SCALE * inside(sum_v) - col_v) / lay
@@ -659,8 +679,7 @@
     out_tv[...] = inside(flow_v)
     for step in range(STEPS):
         for phase in (RIMS, FORCE, PLANE, EARLY):
-            if phase != EARLY or step:
-                sent(phase, step)
+            sent(phase, step)
 
 
 def per_device(velocity_u, velocity_v, buoyancy, surface, transport_u, transport_v, ocean, layers):
@@ -699,12 +718,12 @@
             pltpu.VMEM((STEPS, 2, ROWS, LANES), F32),
             pltpu.VMEM((STEPS, 2, RIM, LANES), F32),
             pltpu.VMEM((STEPS, 6, ROWS, LANES), F32),
-            pltpu.VMEM((STEPS, 4 * ROWS, LANES), F32),
+            pltpu.VMEM((STEPS, 3 * ROWS, LANES), F32),
             pltpu.VMEM((STEPS, 2, 8, LANES), F32),
-            pltpu.VMEM((STEPS, 2, 4 * ROWS, LANES), F32),
+            pltpu.VMEM((STEPS, 2, 3 * ROWS, LANES), F32),
             pltpu.VMEM((STEPS, 6, 8, LANES), F32),
             pltpu.VMEM((STEPS, 2 * ROWS, LANES), F32),
-            pltpu.VMEM((STEPS, 2, 8, LANES), F32),
+            pltpu.VMEM((STEPS, 8, LANES), F32),
             pltpu.VMEM((STEPS, 2, 2 * ROWS, LANES), F32),
             pltpu.VMEM((STEPS, 6, 8, LANES), F32),
             pltpu.SemaphoreType.DMA((8,)),

time: 24.1 us -> 23.6 us (0.979)
  Pallas kernels: 23.3 us -> 22.7 us
    pallas_call x1, Pallas kernels: 22.5 us -> 21.9 us  [per_device(): pl.pallas_call(kernel, out_shape=outs, in_specs=[hbm] * 8, out_specs=(vme...]
where the time goes in v5:
time: 23.6 us; the launch traced here: 23.4 us
  Pallas kernels  22.7 us (96%)
  between operations  0.64 us (3%)
    pallas_call x1, Pallas kernels, per_device(): pl.pallas_call(kernel, out_shape=outs, in_specs=[hbm] * 8, out_specs=(vme...  21.9 us
    pallas_call x1, Pallas kernels, per_device(): pl.pallas_call(store_kernel, out_shape=outs, in_specs=[vmem] * 6, out_spe...  0.8 us

profile of v5, /device:TPU:1, one launch (start us, length us, event | category | flops | bytes accessed | tf_op | source)
XLA Modules:
  0.0 23.4 jit_solution(11610887995136835948)
XLA Ops:
  0.6 21.9 %shard_map.127 = (f32[16,16,128]{2,1,0:T(8,128)S(1)}, f32[16,16,128]{2,1,0:T(8,128)S(1)}, f32[16,16,128]{2,1,0:T(8,128)S(1)}, f32[16,128]{1,0:T(8,128)S(1)}, f32...) custom-call(f32[16,16,128]{2,1,0:T(8,128)} %vel_u.1, f32[16,16,128]{2,1,0:T(8,128)} %vel_v.1, f32[16,16,128]{2,1,0:T(8,128)} %buoy.1, ...), custom_call_target="tpu_custom_call" | custom-call | tf_op jit(solution)/shard_map/pallas_call | solution.py:696
  22.6 0.8 %shard_map.128 = (f32[16,16,128]{2,1,0:T(8,128)}, f32[16,16,128]{2,1,0:T(8,128)}, f32[16,16,128]{2,1,0:T(8,128)}, f32[16,128]{1,0:T(8,128)}, f32[16,128]{1,0:T(8,128)}, /*index=5*/f32[16,128]{1,0:T(8,128)}) custom-call(f32[16,16,128]{2,1,0:T(8,128)S(1)} %get-tuple-element.12.refs_0_, f32[16,16,128]{2,1,0:T(8,128)S(1)} %get-tuple-element.13.refs_1_, ...), custom_call_target="tpu_custom_call" | custom-call | tf_op jit(solution)/shard_map/pallas_call | solution.py:738

commit v6 on v5

--- a/solution.py
+++ b/solution.py
@@ -21,15 +21,18 @@
 DIRS = [(-1, 0), (1, 0), (0, -1), (0, 1), (-1, -1), (-1, 1), (1, -1), (1, 1)]
 SIDES = [(-1, -1), (0, -1), (1, -1), (-1, 1), (0, 1), (1, 1)]
 MOVING = 2 * LEVELS
-FLAT_ROW = 2 * MOVING
-BUOY_NEAR = FLAT_ROW + 8
+FLAT_ROW = 0
+MOM_NEAR = FLAT_ROW + 8
+MOM_FAR = MOM_NEAR + MOVING
+BUOY_NEAR = MOM_FAR + MOVING
 BUOY_FAR = BUOY_NEAR + LEVELS
 CODE_PLANE = BUOY_FAR + LEVELS
 RIM = CODE_PLANE + ROWS
 HALF = LANES // 2
 
 
-RIMS, FORCE, PLANE, EARLY = 0, 1, 2, 3
+RIMS, FORCE, PLANE, EARLY, CUBES = 0, 1, 2, 3, 4
+PHASES = 5
 EXT = 32
 OWN = 8
 SCALE = LEVELS / SUB
@@ -208,12 +211,14 @@
                 elif phase == PLANE:
                     src, dst = gx_send.at[step], gx_recv.at[step, dst_at]
                 else:
-                    if step == 0:
-                        rows = pl.ds(0, BUOY_FAR) if phase == RIMS else pl.ds(BUOY_FAR, RIM - BUOY_FAR)
-                    elif phase == EARLY:
-                        rows = pl.ds(BUOY_NEAR, 2 * LEVELS)
-                    else:
-                        rows = pl.ds(0, BUOY_NEAR)
+                    first, end = {
+                        (RIMS, 0): (FLAT_ROW, MOM_NEAR),
+                        (CUBES, 0): (MOM_NEAR, BUOY_FAR),
+                        (EARLY, 0): (BUOY_FAR, RIM),
+                        (RIMS, 1): (FLAT_ROW, BUOY_NEAR),
+                        (EARLY, 1): (BUOY_NEAR, CODE_PLANE),
+                    }[phase, min(step, 1)]
+                    rows = pl.ds(first, end - first)
                     src, dst = x_send.at[step, src_at, rows], x_recv.at[step, dst_at, rows]
             else:
                 src_at, dst_at = (0 if d[1] < 0 else 1), SIDES.index(back)
@@ -221,7 +226,7 @@
                     src, dst = fy_send.at[step], fy_recv.at[step, dst_at]
                 elif phase == PLANE:
                     src, dst = gy_send.at[step, src_at], gy_recv.at[step, dst_at]
-                elif phase == (RIMS if step else EARLY):
+                elif phase == CUBES or phase == (RIMS if step else EARLY):
                     continue
                 else:
                     src, dst = y_send.at[step, src_at], y_recv.at[step, dst_at]
@@ -294,7 +299,7 @@
         return to_left, to_right
 
     def put_v(step, j, cells, strips):
-        return put(step, j, j, MOVING + j, cells, strips)
+        return put(step, j, MOM_NEAR + j, MOM_FAR + j, cells, strips)
 
     def put_b(step, k, cells, strips):
         j = MOVING + k
@@ -364,8 +369,10 @@
     for side in range(2):
         x_send[0, side, pl.ds(CODE_PLANE, ROWS)] = code
     start_far(RIMS, 0)
+    start_far(CUBES, 0)
+    start_near(RIMS, 0)
     stage_own(mom_in, 0, MOVING, fx)
-    start_near(RIMS, 0)
+    start_near(CUBES, 0)
     start(EARLY, 0)
     stage_own(buoy_in, MOVING, LEVELS, fx)
 
@@ -391,10 +398,11 @@
         return cyclic(tile[ROWS : 2 * ROWS], tile[2 * ROWS : 2 * ROWS + 8], tile[8:ROWS])
 
     for step in range(STEPS):
-        if step == 0:
-            arrive(RIMS, step)
-        else:
-            arrive(RIMS, step)
+        if step:
+            flats = [inside(c) for c in substep(eta, flow_u, flow_v, wet, depth)]
+            send_plane(step, flats)
+        arrive(RIMS, step)
+        if step:
             arrive(EARLY, step)
         left24 = cyclic(y_recv[step, 1], y_recv[step, 2, 0:8], y_recv[step, 0, 8:16])
         right24 = cyclic(y_recv[step, 4], y_recv[step, 5, 0:8], y_recv[step, 3, 8:16])
@@ -408,113 +416,6 @@
             code_far = lane_pair(odd, far, 2 * STACK, 2 * STACK + 1)
             code_inner = lane_pair(odd, code, LANES - 1, 0)
             act_near = level24 < code_near
-        else:
-            shift_side = [
-                (SCALE * side24(total) - beside_columns(left24, right24, STACK + 1 + a))
-                / jnp.maximum(code_side, 1.0)
-                for a, total in enumerate((sum_u, sum_v))
-            ]
-
-            def couple_pairs(cells, near_code, rows, levels, even_at, odd_at, sources):
-                parity = odd24[0:rows]
-                shift = jnp.where(
-                    is_u24[0:rows],
-                    lane_pair(parity, sources[0][0:rows], even_at, odd_at),
-                    lane_pair(parity, sources[1][0:rows], even_at, odd_at),
-                )
-                moved = jnp.where(levels < near_code, cells + shift, 0.0)
-                return jnp.where(moving24[0:rows], moved, cells)
-
-            near24 = couple_pairs(
-                near24, code_near, ROWS + 8, level24, 0, LANES - 1, shift_side
-            )
-            far = couple_pairs(far, code_far, ROWS, level_pair, 1, LANES - 2, shift_side)
-            inner = couple_pairs(
-                inner, code_inner, ROWS, level_pair, LANES - 1, 0, (shift_u, shift_v)
-            )
-            level16 = lax.broadcasted_iota(jnp.int32, (LEVELS, LANES), 0).astype(F32)
-            for side in range(2):
-                for away in range(2):
-                    at = (ROWS - 1 - away, 2 * ROWS + away)[side]
-                    code_row = x_recv[0, side, pl.ds(FLAT_ROW + away, 1)]
-                    for a, total in enumerate((sum_u, sum_v)):
-                        column = x_recv[1, side, pl.ds(FLAT_ROW + 2 * (1 + a) + away, 1)]
-                        shift = (
-                            SCALE * total[at : at + 1, 0:LANES] - column
-                        ) / jnp.maximum(code_row, 1.0)
-                        rows = pl.ds(MOVING * away + LEVELS * a, LEVELS)
-                        rim_new[side, rows] = jnp.where(
-                            level16 < code_row, x_recv[1, side, rows] + shift, 0.0
-                        )
-
-        near_ext[...] = near24
-        near = near24[0:ROWS]
-        lap_near = jnp.where(
-            act_near,
-            turn(near24, 1, 0) + turn(near24, -1, 0) - 4.0 * near24,
-            0.0,
-        )[0:ROWS] + jnp.where(act_near[0:ROWS], far + inner, 0.0)
-
-        def rim_cells(side, first, count, at):
-            if first == 0 and step:
-                return rim_new[side, pl.ds(at, count)]
-            return x_recv[step, side, pl.ds(at, count)]
-
-        def rim_rows(ref, first, count, near_at):
-            row = lax.broadcasted_iota(jnp.int32, (count, LANES), 0)
-            group = lax.broadcasted_iota(jnp.int32, (count, LANES), 1) >> 1
-            for side in range(2):
-                cells = rim_cells(side, first, count, near_at)
-                at = ROWS * count + count * side
-                corner = jnp.broadcast_to(
-                    near_ext[pl.ds((ROWS + 7, ROWS)[side], 1)], (count, LANES)
-                )
-                put_parts(ref, at, count, split(cells), 0)
-                put_parts(ref, at, count, pick(group == first + row, corner), 2)
-                fx[pl.ds(EXT * first + (OWN - 1, OWN + ROWS)[side], count, stride=EXT)] = cells
-
-        def rim_laps(ref, first, count, near_at, far_at):
-            level_of = lax.broadcasted_iota(jnp.int32, (count, LANES), 0) & (LEVELS - 1)
-            for side in range(2):
-                cells = rim_cells(side, first, count, near_at)
-                edge = EXT * first + (OWN, OWN + ROWS - 1)[side]
-                beside = rim_cells(side, first, count, far_at) + fx[
-                    pl.ds(edge, count, stride=EXT)
-                ]
-                lanes_sum = ref[pl.ds(ROWS * count + count * side, count), 0:LANES]
-                code_row = x_recv[0, side, pl.ds(FLAT_ROW, 1)]
-                lap = jnp.where(
-                    level_of.astype(F32) < code_row, beside + lanes_sum - 4.0 * cells, 0.0
-                )
-                lp[pl.ds(EXT * first + (OWN - 1, OWN + ROWS)[side], count, stride=EXT)] = lap
-
-        def laplace(j, source, lanes_sum):
-            at = EXT * j + OWN
-            return (
-                source[pl.ds(at - 1, ROWS)] + source[pl.ds(at + 1, ROWS)]
-                + lanes_sum - 4.0 * source[pl.ds(at, ROWS)]
-            )
-
-        def own_laps(ref, first, count):
-            def one(i, carry):
-                level_at = lax.convert_element_type(i & (LEVELS - 1), F32)
-                lanes_sum = ref[pl.ds(pl.multiple_of(ROWS * i, ROWS), ROWS), 0:LANES]
-                lap = laplace(first + i, fx, lanes_sum)
-                lp[pl.ds(EXT * (first + i) + OWN, ROWS)] = jnp.where(level_at < code, lap, 0.0)
-                return carry
-
-            lax.fori_loop(0, count, one, 0, unroll=True)
-
-        def apply(source, rows, width):
-            return jnp.dot(
-                source[0:rows], lane_w[:, 0:width], preferred_element_type=F32
-            )
-
-        rows_uv, rows_b = MOVING * ROWS, LEVELS * ROWS
-        rim_rows(buoy_in, MOVING, LEVELS, BUOY_NEAR)
-        stage_edge(buoy_in, MOVING, LEVELS, near)
-        buoy_out[...] = apply(buoy_in, rows_b + 2 * LEVELS, 2 * LANES)
-        if step == 0:
             grids = []
             for a, own in enumerate(flats):
                 near_at, far_at = FLAT_ROW + 2 * a, FLAT_ROW + 2 * a + 1
@@ -533,12 +434,118 @@
             flats = [cells[0:ROWS, 0:LANES] for cells in ahead]
             send_plane(step, flats + [code])
         else:
-            flats = [inside(c) for c in substep(eta, flow_u, flow_v, wet, depth)]
-            send_plane(step, flats)
-        rim_rows(mom_in, 0, MOVING, 0)
+            shift_side = [
+                (SCALE * side24(total) - beside_columns(left24, right24, STACK + 1 + a))
+                / jnp.maximum(code_side, 1.0)
+                for a, total in enumerate((sum_u, sum_v))
+            ]
+
+            def couple_pairs(cells, near_code, rows, levels, even_at, odd_at, sources):
+                parity = odd24[0:rows]
+                shift = jnp.where(
+                    is_u24[0:rows],
+                    lane_pair(parity, sources[0][0:rows], even_at, odd_at),
+                    lane_pair(parity, sources[1][0:rows], even_at, odd_at),
+                )
+                moved = jnp.where(levels < near_code, cells + shift, 0.0)
+                return jnp.where(moving24[0:rows], moved, cells)
+
+            near24 = couple_pairs(
+                near24, code_near, ROWS + 8, level24, 0, LANES - 1, shift_side
+            )
+            far = couple_pairs(far, code_far, ROWS, level_pair, 1, LANES - 2, shift_side)
+            inner = couple_pairs(
+                inner, code_inner, ROWS, level_pair, LANES - 1, 0, (shift_u, shift_v)
+            )
+            level16 = lax.broadcasted_iota(jnp.int32, (LEVELS, LANES), 0).astype(F32)
+            for side in range(2):
+                for away in range(2):
+                    at = (ROWS - 1 - away, 2 * ROWS + away)[side]
+                    code_row = x_recv[0, side, pl.ds(FLAT_ROW + away, 1)]
+                    for a, total in enumerate((sum_u, sum_v)):
+                        column = x_recv[1, side, pl.ds(FLAT_ROW + 2 * (1 + a) + away, 1)]
+                        shift = (
+                            SCALE * total[at : at + 1, 0:LANES] - column
+                        ) / jnp.maximum(code_row, 1.0)
+                        at_row = MOVING * away + LEVELS * a
+                        star = x_recv[1, side, pl.ds(MOM_NEAR + at_row, LEVELS)]
+                        rim_new[side, pl.ds(at_row, LEVELS)] = jnp.where(
+                            level16 < code_row, star + shift, 0.0
+                        )
+
+        near_ext[...] = near24
+        near = near24[0:ROWS]
+        lap_near = jnp.where(
+            act_near,
+            turn(near24, 1, 0) + turn(near24, -1, 0) - 4.0 * near24,
+            0.0,
+        )[0:ROWS] + jnp.where(act_near[0:ROWS], far + inner, 0.0)
+
+        def rim_cells(side, first, count, at):
+            if first == 0 and step:
+                return rim_new[side, pl.ds(at - MOM_NEAR, count)]
+            return x_recv[step, side, pl.ds(at, count)]
+
+        def rim_rows(ref, first, count, near_at):
+            row = lax.broadcasted_iota(jnp.int32, (count, LANES), 0)
+            group = lax.broadcasted_iota(jnp.int32, (count, LANES), 1) >> 1
+            for side in range(2):
+                cells = rim_cells(side, first, count, near_at)
+                at = ROWS * count + count * side
+                corner = jnp.broadcast_to(
+                    near_ext[pl.ds((ROWS + 7, ROWS)[side], 1)], (count, LANES)
+                )
+                put_parts(ref, at, count, split(cells), 0)
+                put_parts(ref, at, count, pick(group == first + row, corner), 2)
+                fx[pl.ds(EXT * first + (OWN - 1, OWN + ROWS)[side], count, stride=EXT)] = cells
+
+        def rim_laps(ref, first, count, near_at, far_at):
+            level_of = lax.broadcasted_iota(jnp.int32, (count, LANES), 0) & (LEVELS - 1)
+            for side in range(2):
+                cells = rim_cells(side, first, count, near_at)
+                edge = EXT * first + (OWN, OWN + ROWS - 1)[side]
+                beside = rim_cells(side, first, count, far_at) + fx[
+                    pl.ds(edge, count, stride=EXT)
+                ]
+                lanes_sum = ref[pl.ds(ROWS * count + count * side, count), 0:LANES]
+                code_row = x_recv[0, side, pl.ds(FLAT_ROW, 1)]
+                lap = jnp.where(
+                    level_of.astype(F32) < code_row, beside + lanes_sum - 4.0 * cells, 0.0
+                )
+                lp[pl.ds(EXT * first + (OWN - 1, OWN + ROWS)[side], count, stride=EXT)] = lap
+
+        def laplace(j, source, lanes_sum):
+            at = EXT * j + OWN
+            return (
+                source[pl.ds(at - 1, ROWS)] + source[pl.ds(at + 1, ROWS)]
+                + lanes_sum - 4.0 * source[pl.ds(at, ROWS)]
+            )
+
+        def own_laps(ref, first, count):
+            def one(i, carry):
+                level_at = lax.convert_element_type(i & (LEVELS - 1), F32)
+                lanes_sum = ref[pl.ds(pl.multiple_of(ROWS * i, ROWS), ROWS), 0:LANES]
+                lap = laplace(first + i, fx, lanes_sum)
+                lp[pl.ds(EXT * (first + i) + OWN, ROWS)] = jnp.where(level_at < code, lap, 0.0)
+                return carry
+
+            lax.fori_loop(0, count, one, 0, unroll=True)
+
+        def apply(source, rows, width):
+            return jnp.dot(
+                source[0:rows], lane_w[:, 0:width], preferred_element_type=F32
+            )
+
+        rows_uv, rows_b = MOVING * ROWS, LEVELS * ROWS
+        stage_edge(buoy_in, MOVING, LEVELS, near)
         stage_edge(mom_in, 0, MOVING, near)
+        if step == 0:
+            arrive(CUBES, step)
+        rim_rows(buoy_in, MOVING, LEVELS, BUOY_NEAR)
+        buoy_out[...] = apply(buoy_in, rows_b + 2 * LEVELS, 2 * LANES)
+        rim_rows(mom_in, 0, MOVING, MOM_NEAR)
         mom_out[...] = apply(mom_in, rows_uv + 2 * MOVING, LANES)
-        rim_laps(mom_out, 0, MOVING, 0, MOVING)
+        rim_laps(mom_out, 0, MOVING, MOM_NEAR, MOM_FAR)
         own_laps(mom_out, 0, MOVING)
         stage_own(mom_in, 0, MOVING, lp)
         stage_edge(mom_in, 0, MOVING, lap_near)
@@ -678,8 +685,9 @@
     out_tu[...] = inside(flow_u)
     out_tv[...] = inside(flow_v)
     for step in range(STEPS):
-        for phase in (RIMS, FORCE, PLANE, EARLY):
-            sent(phase, step)
+        for phase in range(PHASES):
+            if phase != CUBES or step == 0:
+                sent(phase, step)
 
 
 def per_device(velocity_u, velocity_v, buoyancy, surface, transport_u, transport_v, ocean, layers):
@@ -727,8 +735,8 @@
             pltpu.VMEM((STEPS, 2, 2 * ROWS, LANES), F32),
             pltpu.VMEM((STEPS, 6, 8, LANES), F32),
             pltpu.SemaphoreType.DMA((8,)),
-            pltpu.SemaphoreType.DMA((4 * STEPS, 8)),
-            pltpu.SemaphoreType.DMA((4 * STEPS, 8)),
+            pltpu.SemaphoreType.DMA((PHASES * STEPS, 8)),
+            pltpu.SemaphoreType.DMA((PHASES * STEPS, 8)),
         ],
         compiler_params=pltpu.CompilerParams(
             collective_id=0, has_side_effects=True, vmem_limit_bytes=16 * 2**20

time: 23.6 us -> 22.7 us (0.962)
  Pallas kernels: 22.7 us -> 21.9 us
    pallas_call x1, Pallas kernels: 21.9 us -> 21.1 us  [per_device(): pl.pallas_call(kernel, out_shape=outs, in_specs=[hbm] * 8, out_specs=(vme...]
where the time goes in v6:
time: 22.7 us; the launch traced here: 22.6 us
  Pallas kernels  21.9 us (96%)
  between operations  0.64 us (3%)
    pallas_call x1, Pallas kernels, per_device(): pl.pallas_call(kernel, out_shape=outs, in_specs=[hbm] * 8, out_specs=(vme...  21.1 us
    pallas_call x1, Pallas kernels, per_device(): pl.pallas_call(store_kernel, out_shape=outs, in_specs=[vmem] * 6, out_spe...  0.8 us

profile of v6, /device:TPU:1, one launch (start us, length us, event | category | flops | bytes accessed | tf_op | source)
XLA Modules:
  0.0 22.6 jit_solution(4362119689179035115)
XLA Ops:
  0.6 21.1 %shard_map.127 = (f32[16,16,128]{2,1,0:T(8,128)S(1)}, f32[16,16,128]{2,1,0:T(8,128)S(1)}, f32[16,16,128]{2,1,0:T(8,128)S(1)}, f32[16,128]{1,0:T(8,128)S(1)}, f32...) custom-call(f32[16,16,128]{2,1,0:T(8,128)} %vel_u.1, f32[16,16,128]{2,1,0:T(8,128)} %vel_v.1, f32[16,16,128]{2,1,0:T(8,128)} %buoy.1, ...), custom_call_target="tpu_custom_call" | custom-call | tf_op jit(solution)/shard_map/pallas_call | solution.py:704
  21.8 0.8 %shard_map.128 = (f32[16,16,128]{2,1,0:T(8,128)}, f32[16,16,128]{2,1,0:T(8,128)}, f32[16,16,128]{2,1,0:T(8,128)}, f32[16,128]{1,0:T(8,128)}, f32[16,128]{1,0:T(8,128)}, /*index=5*/f32[16,128]{1,0:T(8,128)}) custom-call(f32[16,16,128]{2,1,0:T(8,128)S(1)} %get-tuple-element.12.refs_0_, f32[16,16,128]{2,1,0:T(8,128)S(1)} %get-tuple-element.13.refs_1_, ...), custom_call_target="tpu_custom_call" | custom-call | tf_op jit(solution)/shard_map/pallas_call | solution.py:746

commit v7 on v6

--- a/solution.py
+++ b/solution.py
@@ -75,20 +75,25 @@
 
 def pack_flat(arrays):
     lane = lax.broadcasted_iota(jnp.int32, (ROWS, LANES), 1)
-    to_left = to_right = jnp.zeros((ROWS, LANES), F32)
+    group = lane[0:8] >> 4
+    to_left = to_right = jnp.zeros((8, LANES), F32)
     for a, cells in enumerate(arrays):
-        to_right = jnp.where((lane >> 4) == a, turn(cells, 16 * a + 16, 1), to_right)
-        to_left = jnp.where((lane >> 4) == a, turn(cells, 16 * a, 1), to_left)
-    return fold(to_left), fold(to_right)
+        for half in range(2):
+            part, at = cells[8 * half : 8 * half + 8], a + 4 * half
+            to_right = jnp.where(group == at, turn(part, 16 * at + 16, 1), to_right)
+            to_left = jnp.where(group == at, turn(part, 16 * at, 1), to_left)
+    return to_left, to_right
 
 
 def wide(own, up, down, sides, a):
-    lane = lax.broadcasted_iota(jnp.int32, (ROWS, LANES), 1)
+    lane = lax.broadcasted_iota(jnp.int32, (8, LANES), 1)
     blocks = []
     for r in range(3):
-        from_left, from_right = unfold(sides[r]), unfold(sides[r + 3])
-        left, right = turn(from_left, 112 - 16 * a, 1), turn(from_right, -16 * a, 1)
-        blocks.append(jnp.where(lane < 16, right, jnp.where(lane >= 112, left, 0.0)))
+        for half in range(2):
+            at = a + 4 * half
+            left = turn(sides[r], 112 - 16 * at, 1)
+            right = turn(sides[r + 3], -16 * at, 1)
+            blocks.append(jnp.where(lane < 16, right, jnp.where(lane >= 112, left, 0.0)))
     main = jnp.concatenate([up, own, down], axis=0)
     return jnp.concatenate([main, jnp.concatenate(blocks, axis=0)], axis=1)
 
@@ -104,7 +109,18 @@
     return eta, wet * new_u, wet * new_v
 
 
-def barotropic(state, push, wet, depth):
+def substep_once(eta, tu, tv, wet, depth, push, wet_ahead, wet_behind):
+    mid = eta - 0.125 * (turn(tu, -1, 0) - turn(tu, 1, 0))
+    ahead = wet_ahead * (turn(mid, -1, 1) - 0.125 * (turn(tv, -2, 1) - tv))
+    behind = wet_behind * (turn(mid, 1, 1) - 0.125 * (tv - turn(tv, 2, 1)))
+    eta = wet * (mid - 0.125 * (turn(tv, -1, 1) - turn(tv, 1, 1)))
+    thick = 0.125 * (depth + eta)
+    new_u = 0.98 * tu - thick * (turn(eta, -1, 0) - turn(eta, 1, 0)) + 0.05 * tv + push[0]
+    new_v = 0.98 * tv - thick * (ahead - behind) - 0.05 * tu + push[1]
+    return eta, wet * new_u, wet * new_v
+
+
+def barotropic(state, push, wet, depth, tail):
     eta, tu, tv = state
     tu, tv = tu + wet * push[0], tv + wet * push[1]
 
@@ -113,7 +129,19 @@
         eta, tu, tv = substep(eta, tu, tv, wet, depth, push)
         return eta, tu, tv, sum_u + tu, sum_v + tv
 
-    return lax.fori_loop(0, SUB - 1, one, (eta, tu, tv, tu, tv), unroll=True)
+    cells = lax.fori_loop(0, SUB - 1 - tail, one, (eta, tu, tv, tu, tv), unroll=True)
+    kept = slice(8, 2 * ROWS + 8)
+    wet, depth = wet[kept], depth[kept]
+    push = [part[kept] for part in push]
+    beside = turn(wet, -1, 1), turn(wet, 1, 1)
+
+    def last(_, carry):
+        eta, tu, tv, sum_u, sum_v = carry
+        eta, tu, tv = substep_once(eta, tu, tv, wet, depth, push, *beside)
+        return eta, tu, tv, sum_u + tu, sum_v + tv
+
+    cells = lax.fori_loop(0, tail, last, tuple(part[kept] for part in cells), unroll=True)
+    return tuple(jnp.concatenate([part[-8:], part, part[0:8]], axis=0) for part in cells)
 
 
 def inside(cells):
@@ -147,7 +175,7 @@
     out_u, out_v, out_b, out_eta, out_tu, out_tv,
     star_u, star_v,
     fx, lp, near_ext, ring_rows, rim_new, in_3d, in_2d, in_int,
-    lane_w, mom_in, buoy_in, mom_out, buoy_out,
+    lane_w, mom_in, buoy_in, mom_out, buoy_out, mom_edge,
     x_send, y_send, x_recv, y_recv, gx_send, gy_send, gx_recv, gy_recv,
     fx_send, fy_send, fx_recv, fy_recv, in_sem, send_sem, recv_sem,
 ):
@@ -287,16 +315,22 @@
     rim_lanes = jnp.logical_or(lane < 16, lane >= LANES - 16)
     zero = jnp.zeros((ROWS, LANES), F32)
 
-    def put(step, j, near_at, far_at, cells, strips):
+    def put_rows(step, near_at, far_at, cells):
         x_send[step, 0, pl.ds(near_at, 1)] = cells[0:1]
         x_send[step, 0, pl.ds(far_at, 1)] = cells[1:2]
         x_send[step, 1, pl.ds(near_at, 1)] = cells[ROWS - 1 : ROWS]
         x_send[step, 1, pl.ds(far_at, 1)] = cells[ROWS - 2 : ROWS - 1]
+
+    def put_strip(j, cells, strips):
         to_left, to_right = strips
         rolled = turn(cells, 2 * j + 2, 1)
         to_right = jnp.where(pair == j, rolled, to_right)
         to_left = jnp.where(pair == j + 1, rolled, to_left)
         return to_left, to_right
+
+    def put(step, j, near_at, far_at, cells, strips):
+        put_rows(step, near_at, far_at, cells)
+        return put_strip(j, cells, strips)
 
     def put_v(step, j, cells, strips):
         return put(step, j, MOM_NEAR + j, MOM_FAR + j, cells, strips)
@@ -332,6 +366,18 @@
             return carry
 
         lax.fori_loop(0, count, one, 0, unroll=True)
+
+    def own_product(source, rows):
+        return jnp.dot(
+            source[0:rows, 0 : 2 * LANES], lane_w[0 : 2 * LANES, 0:LANES],
+            preferred_element_type=F32,
+        )
+
+    def edge_product(source, rows):
+        return jnp.dot(
+            source[0:rows, 2 * LANES : 4 * LANES], lane_w[2 * LANES : 4 * LANES, 0:LANES],
+            preferred_element_type=F32,
+        )
 
     def stage_edge(ref, first, count, edge):
         def one(i, carry):
@@ -372,6 +418,7 @@
     start_far(CUBES, 0)
     start_near(RIMS, 0)
     stage_own(mom_in, 0, MOVING, fx)
+    mom_out[0 : MOVING * ROWS] = own_product(mom_in, MOVING * ROWS)
     start_near(CUBES, 0)
     start(EARLY, 0)
     stage_own(buoy_in, MOVING, LEVELS, fx)
@@ -432,6 +479,8 @@
                 *grids[1:], (grids[0] > 0.0).astype(F32), grids[0] / LEVELS
             )
             flats = [cells[0:ROWS, 0:LANES] for cells in ahead]
+            stage_edge(mom_in, 0, MOVING, near24[0:ROWS])
+            stage_edge(buoy_in, MOVING, LEVELS, near24[0:ROWS])
             send_plane(step, flats + [code])
         else:
             shift_side = [
@@ -524,7 +573,10 @@
         def own_laps(ref, first, count):
             def one(i, carry):
                 level_at = lax.convert_element_type(i & (LEVELS - 1), F32)
-                lanes_sum = ref[pl.ds(pl.multiple_of(ROWS * i, ROWS), ROWS), 0:LANES]
+                at = pl.ds(pl.multiple_of(ROWS * i, ROWS), ROWS)
+                lanes_sum = ref[at, 0:LANES]
+                if first == 0:
+                    lanes_sum = lanes_sum + mom_edge[at]
                 lap = laplace(first + i, fx, lanes_sum)
                 lp[pl.ds(EXT * (first + i) + OWN, ROWS)] = jnp.where(level_at < code, lap, 0.0)
                 return carry
@@ -537,14 +589,18 @@
             )
 
         rows_uv, rows_b = MOVING * ROWS, LEVELS * ROWS
-        stage_edge(buoy_in, MOVING, LEVELS, near)
-        stage_edge(mom_in, 0, MOVING, near)
+        if step:
+            stage_edge(mom_in, 0, MOVING, near)
+            stage_edge(buoy_in, MOVING, LEVELS, near)
         if step == 0:
             arrive(CUBES, step)
+        rim_rows(mom_in, 0, MOVING, MOM_NEAR)
+        mom_edge[...] = edge_product(mom_in, rows_uv)
+        mom_out[pl.ds(rows_uv, 2 * MOVING)] = jnp.dot(
+            mom_in[pl.ds(rows_uv, 2 * MOVING)], lane_w[:, 0:LANES], preferred_element_type=F32
+        )
         rim_rows(buoy_in, MOVING, LEVELS, BUOY_NEAR)
         buoy_out[...] = apply(buoy_in, rows_b + 2 * LEVELS, 2 * LANES)
-        rim_rows(mom_in, 0, MOVING, MOM_NEAR)
-        mom_out[...] = apply(mom_in, rows_uv + 2 * MOVING, LANES)
         rim_laps(mom_out, 0, MOVING, MOM_NEAR, MOM_FAR)
         own_laps(mom_out, 0, MOVING)
         stage_own(mom_in, 0, MOVING, lp)
@@ -585,6 +641,9 @@
             sv = act * (v + 0.2 * tend_v)
             star_u[k] = su
             star_v[k] = sv
+            if step < STEPS - 1:
+                put_rows(step + 1, MOM_NEAR + k, MOM_FAR + k, su)
+                put_rows(step + 1, MOM_NEAR + LEVELS + k, MOM_FAR + LEVELS + k, sv)
             return (
                 press_x, press_y, force_u + act * tend_u, force_v + act * tend_v,
                 col_u + su, col_v + sv,
@@ -605,14 +664,17 @@
         )
         start(FORCE, step)
         if step < STEPS - 1:
+            for a, cells in enumerate((col_u, col_v)):
+                at = FLAT_ROW + 2 * (1 + a)
+                put_rows(step + 1, at, at + 1, cells)
+            start_far(RIMS, step + 1)
             def pack_star(k, strips):
-                strips = put_v(step + 1, k, star_u[k], strips)
-                return put_v(step + 1, LEVELS + k, star_v[k], strips)
+                strips = put_strip(k, star_u[k], strips)
+                return put_strip(LEVELS + k, star_v[k], strips)
 
             strips = lax.fori_loop(0, LEVELS, pack_star, (zero, zero), unroll=True)
-            strips = put_flat(step + 1, 1, col_u, strips)
-            strips = put_flat(step + 1, 2, col_v, strips)
-            start_far(RIMS, step + 1)
+            strips = put_strip(STACK + 1, col_u, strips)
+            strips = put_strip(STACK + 2, col_v, strips)
         if step == 0:
             arrive(EARLY, step)
         rim_laps(buoy_out, MOVING, LEVELS, BUOY_NEAR, BUOY_FAR)
@@ -632,8 +694,8 @@
             y_send[step + 1, 0] = strips[0]
             y_send[step + 1, 1] = strips[1]
             start_far(EARLY, step + 1)
+            start_near(EARLY, step + 1)
             start_near(RIMS, step + 1)
-            start_near(EARLY, step + 1)
             stage_own(buoy_in, MOVING, LEVELS, fx)
         arrive(PLANE, step)
         sides = [gy_recv[step, r] for r in range(6)]
@@ -661,7 +723,7 @@
             push.append(0.2 * jnp.concatenate(
                 [jnp.concatenate(main, axis=0), jnp.concatenate(beside[a], axis=0)], axis=1
             ))
-        eta, flow_u, flow_v, sum_u, sum_v = barotropic(state, push, wet, depth)
+        eta, flow_u, flow_v, sum_u, sum_v = barotropic(state, push, wet, depth, 3 if step < STEPS - 1 else 4)
         shift_u = (SCALE * inside(sum_u) - col_u) / lay
         shift_v = (SCALE * inside(sum_v) - col_v) / lay
 
@@ -680,6 +742,7 @@
         lax.fori_loop(0, LEVELS, couple, 0, unroll=True)
         if step < STEPS - 1:
             stage_own(mom_in, 0, MOVING, fx)
+            mom_out[0 : MOVING * ROWS] = own_product(mom_in, MOVING * ROWS)
 
     out_eta[...] = inside(eta)
     out_tu[...] = inside(flow_u)
@@ -722,6 +785,7 @@
             pltpu.VMEM((LEVELS * (ROWS + 2), 4 * LANES), BF16),
             pltpu.VMEM((MOVING * (ROWS + 2), LANES), F32),
             pltpu.VMEM((LEVELS * (ROWS + 2), 2 * LANES), F32),
+            pltpu.VMEM((MOVING * ROWS, LANES), F32),
             pltpu.VMEM((STEPS, 2, RIM, LANES), F32),
             pltpu.VMEM((STEPS, 2, ROWS, LANES), F32),
             pltpu.VMEM((STEPS, 2, RIM, LANES), F32),

time: 22.7 us -> 22.6 us (level)
  no operation moved by 1% of the time
where the time goes in v7:
time: 22.6 us; the launch traced here: 22.4 us
  Pallas kernels  21.8 us (96%)
  between operations  0.64 us (3%)
    pallas_call x1, Pallas kernels, per_device(): pl.pallas_call(kernel, out_shape=outs, in_specs=[hbm] * 8, out_specs=(vme...  21 us
    pallas_call x1, Pallas kernels, per_device(): pl.pallas_call(store_kernel, out_shape=outs, in_specs=[vmem] * 6, out_spe...  0.8 us

profile of v7, /device:TPU:1, one launch (start us, length us, event | category | flops | bytes accessed | tf_op | source)
XLA Modules:
  0.0 22.4 jit_solution(3210021427224827082)
XLA Ops:
  0.6 21.0 %shard_map.127 = (f32[16,16,128]{2,1,0:T(8,128)S(1)}, f32[16,16,128]{2,1,0:T(8,128)S(1)}, f32[16,16,128]{2,1,0:T(8,128)S(1)}, f32[16,128]{1,0:T(8,128)S(1)}, f32...) custom-call(f32[16,16,128]{2,1,0:T(8,128)} %vel_u.1, f32[16,16,128]{2,1,0:T(8,128)} %vel_v.1, f32[16,16,128]{2,1,0:T(8,128)} %buoy.1, ...), custom_call_target="tpu_custom_call" | custom-call | tf_op jit(solution)/shard_map/pallas_call | solution.py:767
  21.6 0.8 %shard_map.128 = (f32[16,16,128]{2,1,0:T(8,128)}, f32[16,16,128]{2,1,0:T(8,128)}, f32[16,16,128]{2,1,0:T(8,128)}, f32[16,128]{1,0:T(8,128)}, f32[16,128]{1,0:T(8,128)}, /*index=5*/f32[16,128]{1,0:T(8,128)}) custom-call(f32[16,16,128]{2,1,0:T(8,128)S(1)} %get-tuple-element.12.refs_0_, f32[16,16,128]{2,1,0:T(8,128)S(1)} %get-tuple-element.13.refs_1_, ...), custom_call_target="tpu_custom_call" | custom-call | tf_op jit(solution)/shard_map/pallas_call | solution.py:810

commit v8 on v7

--- a/solution.py
+++ b/solution.py
@@ -206,7 +206,7 @@
     here = {d: exists(d) for d in DIRS}
     barrier = pltpu.get_barrier_semaphore()
     total_near = jnp.int32(0)
-    for d in DIRS:
+    for d in DIRS[::-1]:
         total_near = total_near + here[d].astype(jnp.int32)
 
         @pl.when(here[d])
@@ -772,8 +772,8 @@
         scratch_shapes=[
             pltpu.VMEM(block, F32),
             pltpu.VMEM(block, F32),
-            pltpu.VMEM((STACK * EXT, LANES), F32),
-            pltpu.VMEM((STACK * EXT, LANES), F32),
+            pltpu.VMEM((STACK * EXT + EXT, LANES), F32),
+            pltpu.VMEM((STACK * EXT + EXT, LANES), F32),
             pltpu.VMEM((ROWS + 8, LANES), F32),
             pltpu.VMEM((4, 8, LANES), F32),
             pltpu.VMEM((2, 2 * MOVING, LANES), F32),

time: 22.6 us -> 22.6 us (level)
  no operation moved by 1% of the time
where the time goes in v8:
time: 22.6 us; the launch traced here: 22.4 us
  Pallas kernels  21.8 us (96%)
  between operations  0.64 us (3%)
    pallas_call x1, Pallas kernels, per_device(): pl.pallas_call(kernel, out_shape=outs, in_specs=[hbm] * 8, out_specs=(vme...  21 us
    pallas_call x1, Pallas kernels, per_device(): pl.pallas_call(store_kernel, out_shape=outs, in_specs=[vmem] * 6, out_spe...  0.8 us

profile of v8, /device:TPU:1, one launch (start us, length us, event | category | flops | bytes accessed | tf_op | source)
XLA Modules:
  0.0 22.4 jit_solution(4455061799283416479)
XLA Ops:
  0.6 21.0 %shard_map.127 = (f32[16,16,128]{2,1,0:T(8,128)S(1)}, f32[16,16,128]{2,1,0:T(8,128)S(1)}, f32[16,16,128]{2,1,0:T(8,128)S(1)}, f32[16,128]{1,0:T(8,128)S(1)}, f32...) custom-call(f32[16,16,128]{2,1,0:T(8,128)} %vel_u.1, f32[16,16,128]{2,1,0:T(8,128)} %vel_v.1, f32[16,16,128]{2,1,0:T(8,128)} %buoy.1, ...), custom_call_target="tpu_custom_call" | custom-call | tf_op jit(solution)/shard_map/pallas_call | solution.py:767
  21.6 0.8 %shard_map.128 = (f32[16,16,128]{2,1,0:T(8,128)}, f32[16,16,128]{2,1,0:T(8,128)}, f32[16,16,128]{2,1,0:T(8,128)}, f32[16,128]{1,0:T(8,128)}, f32[16,128]{1,0:T(8,128)}, /*index=5*/f32[16,128]{1,0:T(8,128)}) custom-call(f32[16,16,128]{2,1,0:T(8,128)S(1)} %get-tuple-element.12.refs_0_, f32[16,16,128]{2,1,0:T(8,128)S(1)} %get-tuple-element.13.refs_1_, ...), custom_call_target="tpu_custom_call" | custom-call | tf_op jit(solution)/shard_map/pallas_call | solution.py:810
